TPU v7x, 32 devices: a whole 2x2x4 slice. The times are simulated.
32 devices in a mesh: seq: 16 (over z, y, x), head: 2 (over core).
Axes of the slice: x: 2, y: 2, z: 4, core: 2. Of those that a mesh axis runs over, the one named last changes fastest.
Arguments:
- tokens: bfloat16 [2, 2048, 768], P(None, 'seq'), may hold values from -6 to 6
- cotangent: bfloat16 [2, 2048, 768], P(None, 'seq'), may hold values from -6 to 6
- masked: int32 [2, 2048], P(None, 'seq'), may hold values from 0 to 1, as said below
- projections: bfloat16 [2, 3, 768, 768], P(None, None, None, 'head'), may hold values from -0.3125 to 0.3125
- projection_bias: bfloat16 [2, 2, 768], P(None, None, 'head'), may hold values from -4 to 4
- conv_taps: bfloat16 [2, 12, 65], P(None, 'head'), may hold values from -1.75 to 1.75
- output_weight: bfloat16 [2, 768, 768], P(None, 'head'), may hold values from -0.4375 to 0.4375
- output_bias: bfloat16 [2, 2, 768], replicated, may hold values from -4 to 4
- norm_gain: bfloat16 [2, 2, 768], replicated, may hold values from 0.5 to 1.5
- norm_shift: bfloat16 [2, 2, 768], replicated, may hold values from -4 to 4
- inner_weight: bfloat16 [2, 768, 3072], P(None, None, 'head'), may hold values from -0.21875 to 0.21875
- inner_bias: bfloat16 [2, 3072], P(None, 'head'), may hold values from -4 to 4
- outer_weight: bfloat16 [2, 3072, 768], P(None, 'head'), may hold values from -0.109375 to 0.109375
Outputs:
- result: float32 [2, 2048, 768], P(None, 'seq')
- grad_tokens: float32 [2, 2048, 768], P(None, 'seq')
- grad_projections: float32 [2, 3, 768, 768], P(None, None, 'seq', 'head')
- grad_projection_bias: float32 [2, 2, 768], P(None, None, 'head')
- grad_conv_taps: float32 [2, 12, 65], P(None, 'head')
- grad_output_weight: float32 [2, 768, 768], P(None, 'head', 'seq')
- grad_output_bias: float32 [2, 2, 768], replicated
- grad_norm_gain: float32 [2, 2, 768], replicated
- grad_norm_shift: float32 [2, 2, 768], replicated
- grad_inner_weight: float32 [2, 768, 3072], P(None, 'seq', 'head')
- grad_inner_bias: float32 [2, 3072], P(None, 'head')
- grad_outer_weight: float32 [2, 3072, 768], P(None, 'head', 'seq')
Inputs may be any that keep to these rules, and one draw needn't show every extreme that they name: Each sequence has its own share of masked positions, drawn between 5 and 25 percent.
All inputs are finite; a program needn't handle non-finite values.
Results may differ from a plain program's by a relative error of at most 0.03.
Values may be sent and summed in bfloat16 or wider, within the bound.
A program may use at most 192 MiB of HBM per device.

v0:
```python
from functools import partial

import jax
import jax.numpy as jnp
from jax import lax
from jax.sharding import PartitionSpec as P

LANDMARKS = 64
PINV_ITERS = 6
LAYERS = 2


exact_result = lax.Precision.HIGHEST
epsilon = 1e-05


def extended(block, sides, width):
    for axis, dim in sides:
        count = lax.axis_size(axis)
        forward = [(i, i + 1) for i in range(count - 1)]
        backward = [(target, source) for source, target in forward]
        low = lax.ppermute(
            lax.slice_in_dim(block, block.shape[dim] - width, None, axis=dim), axis, forward
        )
        high = lax.ppermute(lax.slice_in_dim(block, 0, width, axis=dim), axis, backward)
        block = jnp.concatenate([low, block, high], axis=dim)
    return block


def layer_norm(values, scaling, offset):
    centre = jnp.mean(values, -1, keepdims=True)
    centred = values - centre
    spread = jnp.mean(centred * centred, -1, keepdims=True)
    return centred * lax.rsqrt(spread + epsilon) * scaling + offset


def soft_rows(scores):
    highest = jnp.max(scores, -1, keepdims=True)
    powers = jnp.exp(scores - highest)
    return powers / jnp.sum(powers, -1, keepdims=True)


def pseudo_inverse(weight_matrix):
    size_of = weight_matrix.shape[-1]
    column_top = jnp.max(jnp.sum(weight_matrix, axis=-2), axis=-1)[..., None, None]
    approximate_result = jnp.swapaxes(weight_matrix, -1, -2) / column_top
    identity = jnp.eye(size_of, dtype=jnp.float32)
    for repeat in range(PINV_ITERS):
        product = jnp.matmul(weight_matrix, approximate_result, precision=exact_result)
        nested = 7.0 * identity - product
        nested = 15.0 * identity - jnp.matmul(product, nested, precision=exact_result)
        nested = 13.0 * identity - jnp.matmul(product, nested, precision=exact_result)
        approximate_result = 0.25 * jnp.matmul(approximate_result, nested, precision=exact_result)
    return approximate_result


def rounded(values):
    return lax.optimization_barrier(values.astype(jnp.bfloat16)).astype(jnp.float32)


def heads_view(joined, heads_local):
    batch_count, length, channels = joined.shape
    return joined.reshape(batch_count, length, heads_local, channels // heads_local).transpose(
        0, 2, 1, 3
    )


def tokens_view(by_head):
    batch_count, heads_local, length, head_depth = by_head.shape
    return by_head.transpose(0, 2, 1, 3).reshape(batch_count, length, heads_local * head_depth)


def convolve(padded, broad_kernel_taps, length):

    def add_tap(offset, running):
        window = lax.dynamic_slice_in_dim(padded, offset, length, 1).astype(jnp.float32)
        return running + window * lax.dynamic_index_in_dim(broad_kernel_taps, offset, 0, False)

    initial = jnp.zeros((padded.shape[0], length, padded.shape[2]), jnp.float32)
    return lax.fori_loop(0, broad_kernel_taps.shape[0], add_tap, initial)


def tap_sums(padded, upstream, length, kernel):

    def one_tap(offset):
        window = lax.dynamic_slice_in_dim(padded, offset, length, 1).astype(jnp.float32)
        return jnp.sum(window * upstream, axis=(0, 1))

    return lax.map(one_tap, jnp.arange(kernel, dtype=jnp.int32))


def across_heads(summand):
    return lax.psum_scatter(
        summand.astype(jnp.bfloat16), "head", scatter_dimension=0, tiled=True
    ).astype(jnp.float32)


def rows_low(share):
    return lax.all_gather(share, "head", axis=0, tiled=True)


def rows_float(share):
    return lax.all_gather(share.astype(jnp.bfloat16), "head", axis=0, tiled=True).astype(
        share.dtype
    )


def own_rows(whole_rows):
    share = whole_rows.shape[0] // lax.axis_size("head")
    return lax.dynamic_slice_in_dim(whole_rows, lax.axis_index("head") * share, share, 0)


def spread_heads(share, dim_index):
    groups = lax.axis_size("head")
    full_shape = list(share.shape)
    full_shape[dim_index] = full_shape[dim_index] * groups
    empty = jnp.zeros(full_shape, jnp.float32)
    return lax.dynamic_update_slice_in_dim(
        empty, share, lax.axis_index("head") * share.shape[dim_index], dim_index
    )


def own_heads(whole, width, dim_index):
    return lax.dynamic_slice_in_dim(whole, lax.axis_index("head") * width, width, dim_index)


def forward_layer(hidden, weights, selector, segment):
    (
        projection,
        projection_shift,
        conv_kernel,
        output_matrix,
        output_shift,
        gain_pair,
        shift_pair,
        inner_matrix,
        inner_shift,
        outer_matrix,
    ) = weights
    batch_count, length, model_width = hidden.shape
    heads_local = conv_kernel.shape[0]
    kernel = conv_kernel.shape[1]
    margin = kernel // 2
    local_width = projection.shape[2]
    head_depth = local_width // heads_local
    scale = float(head_depth) ** (-0.25)
    hidden_low = hidden.astype(jnp.bfloat16).reshape(batch_count * length, model_width)
    projected = jnp.einsum(
        "nd,kde->kne", hidden_low, projection, preferred_element_type=jnp.float32
    )
    biases = projection_shift.astype(jnp.float32)
    query_rows = ((projected[0] + biases[0]) * scale).reshape(batch_count, length, local_width)
    key_rows = (projected[1] * scale).reshape(batch_count, length, local_width)
    value_low = (
        (projected[2] + biases[1]).astype(jnp.bfloat16).reshape(batch_count, length, local_width)
    )
    query_sums, key_sums = lax.psum(
        (
            jnp.einsum("mt,btc->bmc", selector, query_rows, precision=exact_result),
            jnp.einsum("mt,btc->bmc", selector, key_rows, precision=exact_result),
        ),
        "seq",
    )
    query_marks = heads_view(query_sums / segment, heads_local)
    key_marks = heads_view(key_sums / segment, heads_local)
    query_heads = heads_view(query_rows, heads_local)
    key_heads = heads_view(key_rows, heads_local)
    value_heads = heads_view(value_low.astype(jnp.float32), heads_local)
    mark_weights = soft_rows(
        jnp.einsum("bhme,bhne->bhmn", query_marks, key_marks, precision=exact_result)
    )
    inverse = pseudo_inverse(mark_weights)
    row_weights = soft_rows(
        jnp.einsum("bhte,bhme->bhtm", query_heads, key_marks, precision=exact_result)
    )
    key_scores = jnp.einsum("bhme,bhte->bhmt", query_marks, key_heads, precision=exact_result)
    local_top = jnp.max(key_scores, -1)
    score_top = lax.pmax(local_top, "seq")
    powers = jnp.exp(key_scores - score_top[..., None])
    neighbour_mixture = jnp.einsum("bhmt,bhte->bhme", powers, value_heads, precision=exact_result)
    score_total, mixed_joined = lax.psum(
        (jnp.sum(powers, -1), neighbour_mixture.reshape(batch_count, heads_local, -1)), "seq"
    )
    mixed_sum = mixed_joined.reshape(neighbour_mixture.shape)
    log_total = score_top + jnp.log(score_total)
    mixed = mixed_sum / score_total[..., None]
    core = jnp.einsum("bhmn,bhne->bhme", inverse, mixed, precision=exact_result)
    attended = jnp.einsum("bhtm,bhme->bhte", row_weights, core, precision=exact_result)
    padded_values = extended(value_low, (("seq", 1),), margin)
    broad_kernel_taps = jnp.repeat(conv_kernel.astype(jnp.float32), head_depth, axis=0).T
    context = tokens_view(attended) + convolve(padded_values, broad_kernel_taps, length)
    context_low = context.astype(jnp.bfloat16).reshape(batch_count * length, local_width)
    attention_share = across_heads(
        jnp.dot(context_low, output_matrix, preferred_element_type=jnp.float32)
    )
    shifts = output_shift.astype(jnp.float32)
    gains = gain_pair.astype(jnp.float32)
    offsets = shift_pair.astype(jnp.float32)
    hidden_share = own_rows(hidden.reshape(batch_count * length, model_width))
    total_first = hidden_share + attention_share + shifts[0]
    normed = layer_norm(total_first, gains[0], offsets[0])
    normed_low = rows_low(normed.astype(jnp.bfloat16))
    pre_active = jnp.dot(
        normed_low, inner_matrix, preferred_element_type=jnp.float32
    ) + inner_shift.astype(jnp.float32)
    active_low = jax.nn.gelu(pre_active, approximate=False).astype(jnp.bfloat16)
    feed_share = across_heads(jnp.dot(active_low, outer_matrix, preferred_element_type=jnp.float32))
    total_second = normed + feed_share + shifts[1]
    output = rows_float(layer_norm(total_second, gains[1], offsets[1])).reshape(hidden.shape)
    retained = (
        hidden_low,
        query_heads,
        key_heads,
        value_heads,
        padded_values,
        query_marks,
        key_marks,
        mark_weights,
        inverse,
        row_weights,
        log_total,
        mixed,
        core,
        context_low,
        total_first,
        normed_low,
        pre_active,
        active_low,
        total_second,
        broad_kernel_taps,
    )
    return (output, retained)


def backward_layer(upstream, retained, weights, selector, segment):
    (
        projection,
        projection_shift,
        conv_kernel,
        output_matrix,
        output_shift,
        gain_pair,
        shift_pair,
        inner_matrix,
        inner_shift,
        outer_matrix,
    ) = weights
    (
        hidden_low,
        query_heads,
        key_heads,
        value_heads,
        padded_values,
        query_marks,
        key_marks,
        mark_weights,
        inverse,
        row_weights,
        log_total,
        mixed,
        core,
        context_low,
        total_first,
        normed_low,
        pre_active,
        active_low,
        total_second,
        broad_kernel_taps,
    ) = retained
    batch_count, length, model_width = upstream.shape
    heads_local = conv_kernel.shape[0]
    kernel = conv_kernel.shape[1]
    margin = kernel // 2
    local_width = projection.shape[2]
    head_depth = local_width // heads_local
    scale = float(head_depth) ** (-0.25)
    gains = gain_pair.astype(jnp.float32)
    offsets = shift_pair.astype(jnp.float32)
    upstream_share = own_rows(upstream.reshape(batch_count * length, model_width))
    second_pull = jax.vjp(layer_norm, total_second, gains[1], offsets[1])[1]
    grad_second, gain_second, offset_second = second_pull(upstream_share)
    feed_low = rows_low(grad_second.astype(jnp.bfloat16))
    grad_outer = jnp.einsum("nf,nd->fd", active_low, feed_low, preferred_element_type=jnp.float32)
    grad_active = rounded(
        jnp.einsum("nd,fd->nf", feed_low, outer_matrix, preferred_element_type=jnp.float32)
    )
    gelu_pull = jax.vjp(partial(jax.nn.gelu, approximate=False), pre_active)[1]
    grad_pre_low = gelu_pull(grad_active)[0].astype(jnp.bfloat16)
    grad_inner_shift = jnp.sum(grad_pre_low.astype(jnp.float32), axis=0)
    grad_inner = jnp.einsum(
        "nd,nf->df", normed_low, grad_pre_low, preferred_element_type=jnp.float32
    )
    normed_term = jnp.einsum(
        "nf,df->nd", grad_pre_low, inner_matrix, preferred_element_type=jnp.float32
    )
    grad_normed = grad_second + across_heads(normed_term)
    first_pull = jax.vjp(layer_norm, total_first, gains[0], offsets[0])[1]
    grad_first, gain_first, offset_first = first_pull(grad_normed)
    attend_low = rows_low(grad_first.astype(jnp.bfloat16))
    grad_output = jnp.einsum(
        "nc,nd->cd", context_low, attend_low, preferred_element_type=jnp.float32
    )
    grad_context_low = (
        jnp.einsum("nd,cd->nc", attend_low, output_matrix, preferred_element_type=jnp.float32)
        .astype(jnp.bfloat16)
        .reshape(batch_count, length, local_width)
    )
    grad_context = lax.optimization_barrier(grad_context_low).astype(jnp.float32)
    padded_grads = extended(grad_context_low, (("seq", 1),), margin)
    grad_conv_values = convolve(padded_grads, broad_kernel_taps[::-1], length)
    kernel_sums = tap_sums(padded_values, grad_context, length, kernel)
    grad_kernel = kernel_sums.reshape(kernel, heads_local, head_depth).sum(-1).T
    grad_attended = heads_view(grad_context, heads_local)
    grad_row = jnp.einsum("bhte,bhme->bhtm", grad_attended, core, precision=exact_result)
    grad_core_local = jnp.einsum(
        "bhtm,bhte->bhme", row_weights, grad_attended, precision=exact_result
    )
    grad_row_scores = row_weights * (grad_row - jnp.sum(row_weights * grad_row, -1, keepdims=True))
    grad_query = jnp.einsum("bhtm,bhme->bhte", grad_row_scores, key_marks, precision=exact_result)
    grad_keymark_local = jnp.einsum(
        "bhtm,bhte->bhme", grad_row_scores, query_heads, precision=exact_result
    )
    grad_core_joined, grad_keymark_joined = lax.psum(
        (
            grad_core_local.reshape(batch_count, heads_local, -1),
            grad_keymark_local.reshape(batch_count, heads_local, -1),
        ),
        "seq",
    )
    grad_core = grad_core_joined.reshape(core.shape)
    grad_inverse = jnp.einsum("bhme,bhne->bhmn", grad_core, mixed, precision=exact_result)
    grad_mixed = jnp.einsum("bhnm,bhne->bhme", inverse, grad_core, precision=exact_result)
    grad_marks = jax.vjp(pseudo_inverse, mark_weights)[1](grad_inverse)[0]
    grad_mark_scores = mark_weights * (
        grad_marks - jnp.sum(mark_weights * grad_marks, -1, keepdims=True)
    )
    grad_querymark = jnp.einsum(
        "bhmn,bhne->bhme", grad_mark_scores, key_marks, precision=exact_result
    )
    grad_keymark = grad_keymark_joined.reshape(key_marks.shape) + jnp.einsum(
        "bhmn,bhme->bhne", grad_mark_scores, query_marks, precision=exact_result
    )
    key_scores = jnp.einsum("bhme,bhte->bhmt", query_marks, key_heads, precision=exact_result)
    key_weights = jnp.exp(key_scores - log_total[..., None])
    grad_values = jnp.einsum("bhmt,bhme->bhte", key_weights, grad_mixed, precision=exact_result)
    offset_term = jnp.sum(grad_mixed * mixed, -1)
    grad_key_scores = key_weights * (
        jnp.einsum("bhme,bhte->bhmt", grad_mixed, value_heads, precision=exact_result)
        - offset_term[..., None]
    )
    grad_key = jnp.einsum("bhmt,bhme->bhte", grad_key_scores, query_marks, precision=exact_result)
    grad_querymark_local = jnp.einsum(
        "bhmt,bhte->bhme", grad_key_scores, key_heads, precision=exact_result
    )
    grad_querymark = grad_querymark + lax.psum(
        grad_querymark_local.reshape(batch_count, heads_local, -1), "seq"
    ).reshape(query_marks.shape)
    grad_query = (
        grad_query
        + jnp.einsum("mt,bhme->bhte", selector, grad_querymark, precision=exact_result) / segment
    )
    grad_key = (
        grad_key
        + jnp.einsum("mt,bhme->bhte", selector, grad_keymark, precision=exact_result) / segment
    )
    grad_values = grad_values + heads_view(grad_conv_values, heads_local)
    query_low = (
        (tokens_view(grad_query) * scale)
        .astype(jnp.bfloat16)
        .reshape(batch_count * length, local_width)
    )
    key_low = (
        (tokens_view(grad_key) * scale)
        .astype(jnp.bfloat16)
        .reshape(batch_count * length, local_width)
    )
    value_grad_low = (
        tokens_view(grad_values).astype(jnp.bfloat16).reshape(batch_count * length, local_width)
    )
    stacked = jnp.stack([query_low, key_low, value_grad_low])
    grad_projection = jnp.einsum(
        "nd,kne->kde", hidden_low, stacked, preferred_element_type=jnp.float32
    )
    grad_projection_shift = jnp.stack(
        [
            jnp.sum(query_low.astype(jnp.float32), axis=0),
            jnp.sum(value_grad_low.astype(jnp.float32), axis=0),
        ]
    )
    input_term = jnp.einsum("kne,kde->nd", stacked, projection, preferred_element_type=jnp.float32)
    grad_hidden = rows_float(grad_first + across_heads(input_term)).reshape(upstream.shape)
    gradients = (
        grad_projection,
        grad_projection_shift,
        grad_kernel,
        grad_output,
        jnp.stack([jnp.sum(grad_first, axis=0), jnp.sum(grad_second, axis=0)]),
        jnp.stack([gain_first, gain_second]),
        jnp.stack([offset_first, offset_second]),
        grad_inner,
        grad_inner_shift,
        grad_outer,
    )
    return (grad_hidden, gradients)


def on_device(
    tokens,
    cotangent,
    masked,
    projections,
    projection_bias,
    conv_taps,
    output_weight,
    output_bias,
    norm_gain,
    norm_shift,
    inner_weight,
    inner_bias,
    outer_weight,
):
    length = tokens.shape[1]
    segment = length * lax.axis_size("seq") // LANDMARKS
    position = lax.axis_index("seq") * length + jnp.arange(length, dtype=jnp.int32)
    selector = (
        position[None, :] // segment == jnp.arange(LANDMARKS, dtype=jnp.int32)[:, None]
    ).astype(jnp.float32)
    arrays = (
        projections,
        projection_bias,
        conv_taps,
        output_weight,
        output_bias,
        norm_gain,
        norm_shift,
        inner_weight,
        inner_bias,
        outer_weight,
    )
    hidden = tokens.astype(jnp.float32)
    stored = []
    for layer_number in range(LAYERS):
        weights = tuple((tensor[layer_number] for tensor in arrays))
        hidden, retained = forward_layer(hidden, weights, selector, segment)
        stored.append((weights, retained))
    upstream = cotangent.astype(jnp.float32) * masked.astype(jnp.float32)[:, :, None]
    layer_grads = [None] * LAYERS
    for layer_number in range(LAYERS - 1, -1, -1):
        weights, retained = stored[layer_number]
        upstream, gradients = backward_layer(upstream, retained, weights, selector, segment)
        larger = (
            lax.psum_scatter(gradients[0], "seq", scatter_dimension=1, tiled=True),
            lax.psum_scatter(gradients[3], "seq", scatter_dimension=1, tiled=True),
            lax.psum_scatter(gradients[7], "seq", scatter_dimension=0, tiled=True),
            lax.psum_scatter(gradients[9], "seq", scatter_dimension=1, tiled=True),
        )
        gradients = (
            larger[0],
            gradients[1],
            gradients[2],
            larger[1],
            gradients[4],
            gradients[5],
            gradients[6],
            larger[2],
            gradients[8],
            larger[3],
        )
        layer_grads[layer_number] = gradients
    stacked = tuple(
        (
            jnp.stack([layer_grads[layer_number][member] for layer_number in range(LAYERS)])
            for member in range(10)
        )
    )
    larger = (stacked[0], stacked[3], stacked[7], stacked[9])
    bias_width = stacked[1].shape[2]
    taps_width = stacked[2].shape[1]
    inner_width = stacked[8].shape[1]
    smaller = lax.psum(
        (
            spread_heads(stacked[1], 2),
            spread_heads(stacked[2], 1),
            stacked[4],
            stacked[5],
            stacked[6],
            spread_heads(stacked[8], 1),
        ),
        ("seq", "head"),
    )
    grad_bias_share = own_heads(smaller[0], bias_width, 2)
    grad_taps_share = own_heads(smaller[1], taps_width, 1)
    grad_inner_share = own_heads(smaller[5], inner_width, 1)
    return (
        hidden,
        upstream,
        larger[0],
        grad_bias_share,
        grad_taps_share,
        larger[1],
        smaller[2],
        smaller[3],
        smaller[4],
        larger[2],
        grad_inner_share,
        larger[3],
    )


def solution(mesh):
    in_specs = (
        P(None, "seq", None),
        P(None, "seq", None),
        P(None, "seq"),
        P(None, None, None, "head"),
        P(None, None, "head"),
        P(None, "head", None),
        P(None, "head", None),
        P(),
        P(),
        P(),
        P(None, None, "head"),
        P(None, "head"),
        P(None, "head", None),
    )
    out_specs = (
        P(None, "seq", None),
        P(None, "seq", None),
        P(None, None, "seq", "head"),
        P(None, None, "head"),
        P(None, "head", None),
        P(None, "head", "seq"),
        P(),
        P(),
        P(),
        P(None, "seq", "head"),
        P(None, "head"),
        P(None, "head", "seq"),
    )
    return jax.shard_map(
        on_device, mesh=mesh, in_specs=in_specs, out_specs=out_specs, check_vma=False
    )
```

profile of v0, /device:TPU:0, one launch (start us, length us, event | category | flops | bytes accessed | tf_op | source)
XLA Modules:
  0.0 3119.5 jit_solution(833505032727416602)
XLA Ops:
  22.4 101.0 %all-reduce.19.cloned.1.call-done = f32[2,64,384]{2,1,0:T(8,128)} async-done(((f32[2,64,384]{2,1,0:T(8,128)}), f32[2,64,384]{2,1,0:T(8,128)}) %all-reduce.19.cloned.1.call-update) | async-done | bytes 196624 | tf_op jit(solution)/shard_map/psum | solution.py:157
  125.2 40.3 %pmax.14 = f32[2,6,64]{2,1,0:T(8,128)S(1)} all-reduce(f32[2,6,64]{2,1,0:T(8,128)S(1)} %get-tuple-element.625), channel_id=1, replica_groups=mesh['seq'=16,'head'=2] {'seq'}, use_global_device_ids=true, to_apply=%region_9.10 | all-reduce | flops 768 | bytes 6144 | tf_op jit(solution)/shard_map/pmax | solution.py:178
  166.9 15.1 while.78
  182.4 37.2 %psum.143 = f32[2,6,64]{2,1,0:T(8,128)S(1)} all-reduce(f32[2,6,64]{2,1,0:T(8,128)S(1)} %fusion.234), channel_id=1, replica_groups=mesh['seq'=16,'head'=2] {'seq'}, use_global_device_ids=true, to_apply=%region_12.13 | all-reduce | flops 768 | bytes 6144 | tf_op jit(solution)/shard_map/psum | solution.py:181
  219.6 53.3 %all-reduce.37.cloned.1.call-done = (f32[2,64,384]{2,1,0:T(8,128)}, f32[2,6,64,64]{3,2,1,0:T(8,128)}) async-done(((f32[2,64,384]{2,1,0:T(8,128)}, f32[2,6,64,64]{3,2,1,0:T(8,128)}), (f32[2,64,384]{2,1,0:T(8,128)}, f32[2,6,64,64]{3,2,1,0:T(8,128)})) %all-reduce.37.cloned.1.call-update) | async-done | bytes 393232 | tf_op jit(solution)/shard_map/psum | solution.py:157
  377.1 96.0 %all-reduce.21.cloned.1.call-done = f32[2,64,384]{2,1,0:T(8,128)} async-done(((f32[2,64,384]{2,1,0:T(8,128)}), f32[2,64,384]{2,1,0:T(8,128)}) %all-reduce.21.cloned.1.call-update) | async-done | bytes 196624 | tf_op jit(solution)/shard_map/psum | solution.py:157
  476.8 40.3 %pmax.15 = f32[2,6,64]{2,1,0:T(8,128)S(1)} all-reduce(f32[2,6,64]{2,1,0:T(8,128)S(1)} %get-tuple-element.632), channel_id=1, replica_groups=mesh['seq'=16,'head'=2] {'seq'}, use_global_device_ids=true, to_apply=%region_30.31 | all-reduce | flops 768 | bytes 6144 | tf_op jit(solution)/shard_map/pmax | solution.py:178
  519.4 60.8 %while.79 = (s32[]{:T(128)}, f32[2,128,384]{2,1,0:T(8,128)S(1)}, bf16[2,192,384]{2,1,0:T(8,128)(2,1)S(1)}, f32[65,384]{1,0:T(8,128)}, s32[]{:T(128)}, /*index=5*/s32[]{:T(128)}) while((s32[]{:T(128)}, f32[2,128,384]{2,1,0:T(8,128)S(1)}, bf16[2,192,384]{2,1,0:T(8,128)(2,1)S(1)}, f32[65,384]{1,0:T(8,128)}, s32[]{:T(128)}, ...), condition=%wide.region_35.36_spmd.clone, body=%wide.region_34.35_spmd.clone.sunk | while | flops 393219 | bytes 987735 | solution.py:80
  580.6 37.3 %psum.147 = f32[2,6,64]{2,1,0:T(8,128)S(1)} all-reduce(f32[2,6,64]{2,1,0:T(8,128)S(1)} %fusion.238), channel_id=1, replica_groups=mesh['seq'=16,'head'=2] {'seq'}, use_global_device_ids=true, to_apply=%region_33.34 | all-reduce | flops 768 | bytes 6144 | tf_op jit(solution)/shard_map/psum | solution.py:181
  741.0 121.8 %while.80 = (s32[]{:T(128)}, f32[2,128,384]{2,1,0:T(8,128)S(1)}, bf16[2,192,384]{2,1,0:T(8,128)(2,1)}, f32[65,384]{1,0:T(8,128)}, s32[]{:T(128)}, /*index=5*/s32[]{:T(128)}) while((s32[]{:T(128)}, f32[2,128,384]{2,1,0:T(8,128)S(1)}, bf16[2,192,384]{2,1,0:T(8,128)(2,1)}, f32[65,384]{1,0:T(8,128)}, s32[]{:T(128)}, ...), condition=%wide.region_56.57_spmd.clone, body=%wide.region_55.56_spmd.clone.sunk | while | flops 393219 | bytes 987735 | solution.py:80
  922.0 108.9 %all-reduce.33.cloned.1.call-done = (f32[2,6,64,64]{3,2,1,0:T(8,128)}, f32[2,6,64,64]{3,2,1,0:T(8,128)}) async-done(((f32[2,6,64,64]{3,2,1,0:T(8,128)}, f32[2,6,64,64]{3,2,1,0:T(8,128)}), (f32[2,6,64,64]{3,2,1,0:T(8,128)}, f32[2,6,64,64]{3,2,1,0:T(8,128)})) %all-reduce.33.cloned.1.call-update) | async-done | bytes 393232 | tf_op jit(solution)/shard_map/psum | solution.py:323
  1066.5 257.2 %while.77 = (s32[]{:T(128)}, f32[65,384]{1,0:T(8,128)}, s32[65]{0:T(128)S(1)}, bf16[2,192,384]{2,1,0:T(8,128)(2,1)S(1)}, f32[2,128,384]{2,1,0:T(8,128)S(1)}, /*index=5*/s32[]{:T(128)}, s32[]{:T(128)}, s32[]{:T(128)}) while((s32[]{:T(128)}, f32[65,384]{1,0:T(8,128)}, s32[65]{0:T(128)S(1)}, bf16[2,192,384]{2,1,0:T(8,128)(2,1)S(1)}, ...), condition=%wide.region_87.88_spmd, body=%wide.region_85.87_spmd.sunk | while | flops 294533 | bytes 597643 | solution.py:89
  1344.7 240.5 %while.76 = (s32[]{:T(128)}, f32[65,384]{1,0:T(8,128)}, s32[65]{0:T(128)S(1)}, bf16[2,192,384]{2,1,0:T(8,128)(2,1)S(1)}, f32[2,128,384]{2,1,0:T(8,128)S(1)}, /*index=5*/s32[]{:T(128)}, s32[]{:T(128)}, s32[]{:T(128)}) while((s32[]{:T(128)}, f32[65,384]{1,0:T(8,128)}, s32[65]{0:T(128)S(1)}, bf16[2,192,384]{2,1,0:T(8,128)(2,1)S(1)}, ...), condition=%wide.region_83.84_spmd, body=%wide.region_81.83_spmd.sunk | while | flops 294533 | bytes 597643 | solution.py:89
  1598.3 61.2 %while.81 = (s32[]{:T(128)}, f32[2,128,384]{2,1,0:T(8,128)S(1)}, bf16[2,192,384]{2,1,0:T(8,128)(2,1)S(1)}, f32[65,384]{1,0:T(8,128)}, s32[]{:T(128)}, /*index=5*/s32[]{:T(128)}) while((s32[]{:T(128)}, f32[2,128,384]{2,1,0:T(8,128)S(1)}, bf16[2,192,384]{2,1,0:T(8,128)(2,1)S(1)}, f32[65,384]{1,0:T(8,128)}, s32[]{:T(128)}, ...), condition=%wide.region_72.73_spmd.clone, body=%wide.region_71.72_spmd.clone.sunk | while | flops 393219 | bytes 987735 | solution.py:80
  1660.5 35.1 %all-reduce.25.cloned.1.call-done = f32[2,6,64,64]{3,2,1,0:T(8,128)} async-done(((f32[2,6,64,64]{3,2,1,0:T(8,128)}), f32[2,6,64,64]{3,2,1,0:T(8,128)}) %all-reduce.25.cloned.1.call-update) | async-done | bytes 196624 | tf_op jit(solution)/shard_map/psum | solution.py:323
  1743.1 108.4 %all-reduce.31.cloned.1.call-done = (f32[2,6,64,64]{3,2,1,0:T(8,128)}, f32[2,6,64,64]{3,2,1,0:T(8,128)}) async-done(((f32[2,6,64,64]{3,2,1,0:T(8,128)}, f32[2,6,64,64]{3,2,1,0:T(8,128)}), (f32[2,6,64,64]{3,2,1,0:T(8,128)}, f32[2,6,64,64]{3,2,1,0:T(8,128)})) %all-reduce.31.cloned.1.call-update) | async-done | bytes 393232 | tf_op jit(solution)/shard_map/psum | solution.py:323
  1901.2 82.5 %all-reduce.27.cloned.1.call-done = (f32[2,2,768]{2,1,0:T(2,128)}, f32[2,12,65]{2,0,1:T(2,128)}, f32[2,2,768]{2,1,0:T(2,128)}, f32[2,2,768]{2,1,0:T(2,128)}, f32[2,2,768]{2,1,0:T(2,128)}, /*index=5*/f32[2,3072]{1,0:T(2,128)}) async-done(((f32[2,2,768]{2,1,0:T(2,128)}, f32[2,12,65]{2,0,1:T(2,128)}, f32[2,2,768]{2,1,0:T(2,128)}, f32[2,2,768]{2,1,0:T(2,128)}, f32[2,2,768]{2,1,0:T(2,128)}, ...) | async-done | bytes 79984 | tf_op jit(solution)/shard_map/psum | solution.py:480
  1999.4 126.1 %reduce-scatter.33.cloned.1.call-done = f32[384,48]{0,1:T(8,128)} async-done(((f32[384,768]{0,1:T(8,128)}), f32[384,48]{0,1:T(8,128)}) %reduce-scatter.33.cloned.1.call-update) | async-done | bytes 73744 | tf_op jit(solution)/shard_map/reduce_scatter | solution.py:453
  2125.5 128.1 %reduce-scatter.31.cloned.1.call-done = f32[384,48]{0,1:T(8,128)} async-done(((f32[384,768]{0,1:T(8,128)}), f32[384,48]{0,1:T(8,128)}) %reduce-scatter.31.cloned.1.call-update) | async-done | bytes 73744 | tf_op jit(solution)/shard_map/reduce_scatter | solution.py:453
  2255.1 285.0 %all-reduce.29.cloned.1.call-done = (f32[3,768,384]{2,0,1:T(4,128)}, f32[3,768,384]{2,0,1:T(4,128)}) async-done(((f32[3,768,384]{2,0,1:T(4,128)}, f32[3,768,384]{2,0,1:T(4,128)}), (f32[3,768,384]{2,0,1:T(4,128)}, f32[3,768,384]{2,0,1:T(4,128)})) %all-reduce.29.cloned.1.call-update) | async-done | bytes 7077904
  2543.0 138.7 %reduce-scatter.41.cloned.1.call-done = f32[1536,48]{0,1:T(8,128)} async-done(((f32[1536,768]{0,1:T(8,128)}), f32[1536,48]{0,1:T(8,128)}) %reduce-scatter.41.cloned.1.call-update) | async-done | bytes 294928 | tf_op jit(solution)/shard_map/reduce_scatter | solution.py:455
  2681.7 142.6 %reduce-scatter.39.cloned.1.call-done = f32[1536,48]{0,1:T(8,128)} async-done(((f32[1536,768]{0,1:T(8,128)}), f32[1536,48]{0,1:T(8,128)}) %reduce-scatter.39.cloned.1.call-update) | async-done | bytes 294928 | tf_op jit(solution)/shard_map/reduce_scatter | solution.py:455
  2826.2 139.8 %reduce-scatter.37.cloned.1.call-done = f32[48,1536]{1,0:T(8,128)} async-done(((f32[768,1536]{1,0:T(8,128)}), f32[48,1536]{1,0:T(8,128)}) %reduce-scatter.37.cloned.1.call-update) | async-done | bytes 294928 | tf_op jit(solution)/shard_map/reduce_scatter | solution.py:454
  2966.0 142.8 %reduce-scatter.35.cloned.1.call-done = f32[48,1536]{1,0:T(8,128)} async-done(((f32[768,1536]{1,0:T(8,128)}), f32[48,1536]{1,0:T(8,128)}) %reduce-scatter.35.cloned.1.call-update) | async-done | bytes 294928 | tf_op jit(solution)/shard_map/reduce_scatter | solution.py:454
  (2059 shorter events, 1012.8 us)
Async XLA Ops:
  7.2 116.2 %all-reduce.19.cloned.1.call-start = ((), (), s32[]{:S(2)}) async-start(), calls=%async_computation.14 | async-start | bytes 393216 | tf_op jit(solution)/shard_map/psum | solution.py:157
  11.4 261.5 %all-reduce.37.cloned.1.call-start = ((), (), s32[]{:S(2)}) async-start(), calls=%async_computation.37 | async-start | bytes 1179648 | tf_op jit(solution)/shard_map/psum | solution.py:157
  166.8 153.8 %reduce-scatter.15.cloned.1.call-start = ((), (), s32[]{:S(2)}) async-start(), calls=%async_computation.15 | async-start | bytes 589824 | tf_op jit(solution)/shard_map/reduce_scatter | solution.py:93
  313.7 31.5 %reduce-scatter.17.cloned.1.call-start = ((), (), s32[]{:S(2)}) async-start(), calls=%async_computation.16 | async-start | bytes 589824 | tf_op jit(solution)/shard_map/reduce_scatter | solution.py:93
  336.1 136.9 %all-reduce.21.cloned.1.call-start = ((), (), s32[]{:S(2)}) async-start(), calls=%async_computation.17 | async-start | bytes 393216 | tf_op jit(solution)/shard_map/psum | solution.py:157
  363.4 261.7 %all-reduce.35.cloned.1.call-start = ((), (), s32[]{:S(2)}) async-start(), calls=%async_computation.36 | async-start | bytes 1179648 | tf_op jit(solution)/shard_map/psum | solution.py:157
  519.3 147.0 %reduce-scatter.19.cloned.1.call-start = ((), (), s32[]{:S(2)}) async-start(), calls=%async_computation.18 | async-start | bytes 589824 | tf_op jit(solution)/shard_map/reduce_scatter | solution.py:93
  659.5 32.8 %reduce-scatter.21.cloned.1.call-start = ((), (), s32[]{:S(2)}) async-start(), calls=%async_computation.19 | async-start | bytes 589824 | tf_op jit(solution)/shard_map/reduce_scatter | solution.py:93
  683.2 30.8 reduce-scatter.23.cloned.1.call-start
  704.9 158.9 %all-reduce.23.cloned.1.call-start = ((), (), s32[]{:S(2)}) async-start(), calls=%async_computation.21 | async-start | bytes 786432 | tf_op jit(solution)/shard_map/psum | solution.py:323
  729.6 301.3 %all-reduce.33.cloned.1.call-start = ((), (), s32[]{:S(2)}) async-start(), calls=%async_computation.35 | async-start | bytes 1572864 | tf_op jit(solution)/shard_map/psum | solution.py:323
  919.1 132.3 %reduce-scatter.25.cloned.1.call-start = ((), (), s32[]{:S(2)}) async-start(), calls=%async_computation.22 | async-start | bytes 589824 | tf_op jit(solution)/shard_map/reduce_scatter | solution.py:93
  1044.5 284.9 %reduce-scatter.27.cloned.1.call-start = ((), (), s32[]{:S(2)}) async-start(), calls=%async_computation.23 | async-start | bytes 589824 | tf_op jit(solution)/shard_map/reduce_scatter | solution.py:93
  1065.8 629.8 %all-reduce.25.cloned.1.call-start = ((), (), s32[]{:S(2)}) async-start(), calls=%async_computation.24 | async-start | bytes 786432 | tf_op jit(solution)/shard_map/psum | solution.py:323
  1586.4 265.2 %all-reduce.31.cloned.1.call-start = ((), (), s32[]{:S(2)}) async-start(), calls=%async_computation.34 | async-start | bytes 1572864 | tf_op jit(solution)/shard_map/psum | solution.py:323
  1741.9 241.7 %all-reduce.27.cloned.1.call-start = ((), (), s32[]{:S(2)}) async-start(), calls=%async_computation.32 | async-start | bytes 172032 | tf_op jit(solution)/shard_map/psum | solution.py:480
  1861.3 134.1 %reduce-scatter.29.cloned.1.call-start = ((), (), s32[]{:S(2)}) async-start(), calls=%async_computation.25 | async-start | bytes 589824 | tf_op jit(solution)/shard_map/reduce_scatter | solution.py:93
  1864.4 261.1 %reduce-scatter.33.cloned.1.call-start = ((), (), s32[]{:S(2)}) async-start(), calls=%async_computation.27 | async-start | bytes 1253376 | tf_op jit(solution)/shard_map/reduce_scatter | solution.py:453
  1865.9 387.6 %reduce-scatter.31.cloned.1.call-start = ((), (), s32[]{:S(2)}) async-start(), calls=%async_computation.26 | async-start | bytes 1253376 | tf_op jit(solution)/shard_map/reduce_scatter | solution.py:453
  1867.5 672.6 %all-reduce.29.cloned.1.call-start = ((), (), s32[]{:S(2)}) async-start(), calls=%async_computation.33 | async-start | bytes 18874368
  1879.4 802.3 %reduce-scatter.41.cloned.1.call-start = ((), (), s32[]{:S(2)}) async-start(), calls=%async_computation.31 | async-start | bytes 5013504 | tf_op jit(solution)/shard_map/reduce_scatter | solution.py:455
  1883.6 940.7 %reduce-scatter.39.cloned.1.call-start = ((), (), s32[]{:S(2)}) async-start(), calls=%async_computation.30 | async-start | bytes 5013504 | tf_op jit(solution)/shard_map/reduce_scatter | solution.py:455
  1887.8 1078.2 %reduce-scatter.37.cloned.1.call-start = ((), (), s32[]{:S(2)}) async-start(), calls=%async_computation.29 | async-start | bytes 5013504 | tf_op jit(solution)/shard_map/reduce_scatter | solution.py:454
  1892.0 1216.8 %reduce-scatter.35.cloned.1.call-start = ((), (), s32[]{:S(2)}) async-start(), calls=%async_computation.28 | async-start | bytes 5013504 | tf_op jit(solution)/shard_map/reduce_scatter | solution.py:454
  (255 other events, 6200.3 us)
Sparse Core Ops, SparseCore 0:
  13.8 109.5 all-reduce.18
  166.9 105.8 all-reduce.36
  313.8 6.6 reduce-scatter.14
  336.3 8.9 reduce-scatter.16
  363.5 109.5 all-reduce.20
  519.5 105.6 all-reduce.34
  659.6 6.6 reduce-scatter.18
  683.3 8.9 reduce-scatter.20
  705.0 8.9 reduce-scatter.22
  729.7 109.0 all-reduce.22
  919.2 111.6 all-reduce.32
  1044.6 6.7 reduce-scatter.24
  1065.9 8.9 reduce-scatter.26
  1586.5 109.0 all-reduce.24
  1742.0 109.4 all-reduce.30
  1861.4 122.1 all-reduce.26
  1986.4 8.9 reduce-scatter.28
  2000.0 125.4 reduce-scatter.32
  2130.2 123.2 reduce-scatter.30
  2259.7 280.3 all-reduce.28
  2545.3 136.4 reduce-scatter.40
  2687.7 136.5 reduce-scatter.38
  2829.5 136.4 reduce-scatter.36
  2971.9 136.8 reduce-scatter.34
where the time goes:
time: 3160 us; the launch traced here: 3120 us
  waiting for transfers between devices  1740 us (55%)
  local copies, waits for them, and re-layouts  472 us (15%)
  matrix products  256 us (8%)
  loops' own time  243 us (8%)
  other arithmetic  188 us (6%)
  blocking collectives  176 us (6%)
    unnamed x25, waiting for transfers between devices  285 us
    reduce_scatter x2, waiting for transfers between devices, on_device(): lax.psum_scatter(gradients[7], 'seq', scatter_dimension=0, tiled=True)  283 us
    reduce_scatter x2, waiting for transfers between devices, on_device(): lax.psum_scatter(gradients[9], 'seq', scatter_dimension=1, tiled=True)  281 us
    psum x4, waiting for transfers between devices, forward_layer(): lax.psum((jnp.einsum('mt,btc->bmc', selector, query_rows, precision=exact...  258 us
    reduce_scatter x2, waiting for transfers between devices, on_device(): lax.psum_scatter(gradients[3], 'seq', scatter_dimension=1, tiled=True)  254 us
    psum x4, waiting for transfers between devices, backward_layer(): lax.psum((grad_core_local.reshape(batch_count, heads_local, -1), grad_key...  252 us
    another operation x2, loops' own time, tap_sums(): return lax.map(one_tap, jnp.arange(kernel, dtype=jnp.int32))  238 us
    dynamic_update_slice x130, local copies, waits for them, and re-layouts, tap_sums(): return lax.map(one_tap, jnp.arange(kernel, dtype=jnp.int32))  172 us
  transfers between devices with their start and end apart: 32, of which 24 were waited for; matrix products, arithmetic and copies ran while one was open for 15% of the time, Pallas kernels for 0%

commit v1 on v0

--- a/solution.py
+++ b/solution.py
@@ -3,6 +3,8 @@
 import jax
 import jax.numpy as jnp
 from jax import lax
+from jax.experimental import pallas as pl
+from jax.experimental.pallas import tpu as pltpu
 from jax.sharding import PartitionSpec as P
 
 LANDMARKS = 64
@@ -12,6 +14,9 @@
 
 exact_result = lax.Precision.HIGHEST
 epsilon = 1e-05
+
+
+VMEM_LIMIT = 64 * 1024 * 1024 - 128 * 1024
 
 
 def extended(block, sides, width):
@@ -507,6 +512,964 @@
     )
 
 
+F32 = jnp.float32
+BF16 = jnp.bfloat16
+MESH = pl.DeviceIdType.MESH
+
+
+def nn(a, b):
+    return lax.dot_general(a, b, (((1,), (0,)), ((), ())), preferred_element_type=F32)
+
+
+def nt(a, b):
+    return lax.dot_general(a, b, (((1,), (1,)), ((), ())), preferred_element_type=F32)
+
+
+def tn(a, b):
+    return lax.dot_general(a, b, (((0,), (0,)), ((), ())), preferred_element_type=F32)
+
+
+def halves(x):
+    high = x.astype(BF16)
+    return high, (x - high.astype(F32)).astype(BF16)
+
+
+def left3(pair, axis):
+    return jnp.concatenate([pair[0], pair[1], pair[0]], axis=axis)
+
+
+def right3(pair, axis):
+    return jnp.concatenate([pair[0], pair[0], pair[1]], axis=axis)
+
+
+def nn3(a, b):
+    return nn(left3(a, 1), right3(b, 0))
+
+
+def nt3(a, b):
+    return nt(left3(a, 1), right3(b, 1))
+
+
+def tn3(a, b):
+    return tn(left3(a, 0), right3(b, 0))
+
+
+def nn3f(a, b):
+    return nn3(halves(a), halves(b))
+
+
+def nt3f(a, b):
+    return nt3(halves(a), halves(b))
+
+
+def tn3f(a, b):
+    return tn3(halves(a), halves(b))
+
+
+class Fast:
+    def __init__(self, mesh_shape, tokens, conv_taps, inner_weight):
+        self.n = mesh_shape["seq"]
+        self.heads = mesh_shape["head"]
+        self.batch, whole, self.width = tokens.shape
+        self.length = whole // self.n
+        self.layers, all_heads, self.kernel = conv_taps.shape
+        self.local_heads = all_heads // self.heads
+        self.depth = self.width // all_heads
+        self.cols = self.local_heads * self.depth
+        self.hidden = inner_weight.shape[2] // self.heads
+        self.rows = self.batch * self.length
+        self.segment = whole // LANDMARKS
+        self.spans = self.length // self.segment
+        self.units = self.batch * self.local_heads // 2
+        self.bits = self.n.bit_length() - 1
+
+    def fits(self):
+        return (
+            self.n == 1 << self.bits
+            and self.n >= 16
+            and self.heads == 2
+            and self.length == 128
+            and self.batch == 2
+            and self.spans * self.batch == 8
+            and self.depth == 64
+            and self.local_heads % 2 == 0
+            and self.width % (16 * self.n) == 0
+            and self.width % 256 == 0
+            and self.hidden % 512 == 0
+            and self.kernel == 65
+            and self.layers == 2
+            and LANDMARKS == 64
+        )
+
+
+def fused_kernel(
+    z,
+    tok, ups, vec, taps, wp_hbm, wo_hbm, wi_hbm, wf_hbm,
+    result, gtok, gproj, gout, ginner, gouter, gsmall,
+    *,
+    WP, WO, WI, WF,
+    HL, QS, KS, VX, RW, KSC, CTX, T1, T2, NL, GP, ACT, QM, KM, CR, MX, PA, PV, PZ, PC,
+    HID, UP, DT, FL, DPRE, GX, DQ, DK, DV, DP, DQM, DKM, DR, SM, TT, TR,
+    MS, MB, XM, OB, SB, SR, HS, HR, SMR, SMT,
+    G, RV,
+    wsem, hsem_s, hsem_r, msem_s, msem_r, xsem_s, xsem_r, csem_s, csem_r, vsem_s, vsem_r,
+    gsem_s, gsem_r, qsem_s, qsem_r, ssem_s, ssem_r, tsem_s, tsem_r,
+):
+    n, B, L, R, D, C, F = z.n, z.batch, z.length, z.rows, z.width, z.cols, z.hidden
+    U, NP, S, K = z.units, z.local_heads // 2, z.spans, z.kernel
+    CH = D // n
+    NB = z.bits
+    M = LANDMARKS
+    margin = K // 2
+    scale = float(z.depth) ** (-0.25)
+    me = lax.axis_index("seq")
+    core = lax.axis_index("head")
+    first_owner = n // 2 - U // 2
+    is_owner = jnp.logical_and(me >= first_owner, me < first_owner + U)
+    mine = jnp.clip(me - first_owner, 0, U - 1)
+
+    def weight_copies(l):
+        return [
+            pltpu.make_async_copy(wp_hbm.at[l], WP.at[l], wsem.at[l, 0]),
+            pltpu.make_async_copy(wo_hbm.at[l], WO.at[l], wsem.at[l, 1]),
+            pltpu.make_async_copy(wi_hbm.at[l], WI.at[l], wsem.at[l, 2]),
+            pltpu.make_async_copy(wf_hbm.at[l], WF.at[l], wsem.at[l, 3]),
+        ]
+
+    for l in range(z.layers):
+        for c in weight_copies(l):
+            c.start()
+    pltpu.make_async_copy(ups, UP, wsem.at[0, 4]).start()
+
+    barrier = pltpu.get_barrier_semaphore()
+
+    def greet(d, _):
+        pl.semaphore_signal(
+            barrier, inc=1, device_id={"seq": lax.rem(me + d, n)}, device_id_type=MESH
+        )
+        return 0
+
+    lax.fori_loop(1, n, greet, 0)
+    pl.semaphore_signal(barrier, inc=1, device_id={"head": 1 - core}, device_id_type=MESH)
+    pl.semaphore_wait(barrier, n)
+
+    row_id = lax.broadcasted_iota(jnp.int32, (128, 128), 0)
+    lane_id = lax.broadcasted_iota(jnp.int32, (128, 128), 1)
+    low_lane = lane_id < 64
+    low_lane64 = low_lane[0:64]
+    same_head = (row_id < 64) == low_lane
+    eye = row_id == lane_id
+    flip = jnp.where(row_id + lane_id == 127, 1.0, 0.0).astype(BF16)
+
+    def expand(c):
+        return jnp.concatenate(
+            [jnp.where(low_lane64, c, 0.0), jnp.where(low_lane64, 0.0, c)], axis=0
+        )
+
+    def compress(x):
+        return jnp.where(low_lane64, x[0:64], x[64:128])
+
+    def to_row(col):
+        return jnp.sum(jnp.where(eye, col, 0.0), axis=0, keepdims=True)
+
+    def to_col(row):
+        return jnp.sum(jnp.where(eye, row, 0.0), axis=1, keepdims=True)
+
+    def half_sums(x):
+        a = jnp.sum(jnp.where(low_lane, x, 0.0), axis=1, keepdims=True)
+        b = jnp.sum(jnp.where(low_lane, 0.0, x), axis=1, keepdims=True)
+        return jnp.where(low_lane, a, b)
+
+    def half_tops(x):
+        a = jnp.max(jnp.where(low_lane, x, -jnp.inf), axis=1, keepdims=True)
+        b = jnp.max(jnp.where(low_lane, -jnp.inf, x), axis=1, keepdims=True)
+        return jnp.where(low_lane, a, b)
+
+    def unit(u):
+        return u // NP, u % NP
+
+    def tile(ref, l, u):
+        b, j = unit(u)
+        return ref[l, b * L : (b + 1) * L, j * 128 : (j + 1) * 128]
+
+    def pair_tile(ref, l, u):
+        b, j = unit(u)
+        return tuple(
+            ref[l, p, b * L : (b + 1) * L, j * 128 : (j + 1) * 128] for p in range(2)
+        )
+
+    def moments(x):
+        centre = jnp.mean(x, -1, keepdims=True)
+        centred = x - centre
+        spread = jnp.mean(centred * centred, -1, keepdims=True)
+        inverse = lax.rsqrt(spread + epsilon)
+        return centred * inverse, inverse
+
+    def norm_back(x, grad, gain):
+        hat, inverse = moments(x)
+        g = grad * gain
+        a = jnp.mean(g, -1, keepdims=True)
+        b = jnp.mean(g * hat, -1, keepdims=True)
+        total = inverse * (g - a - hat * b)
+        sums = (
+            jnp.sum(grad * hat, axis=0, keepdims=True),
+            jnp.sum(grad, axis=0, keepdims=True),
+            jnp.sum(total, axis=0, keepdims=True),
+        )
+        return total, sums
+
+    def put_small(start, vector):
+        for i in range(vector.shape[1] // 128):
+            SM[start + i : start + i + 1, :] = vector[:, i * 128 : (i + 1) * 128]
+
+    def swap(e):
+        return pltpu.make_async_remote_copy(
+            HS.at[e % 2], HR.at[e % 2], hsem_s.at[e], hsem_r.at[e],
+            device_id={"head": 1 - core}, device_id_type=MESH,
+        )
+
+    def both(e):
+        return HS[e % 2].astype(F32) + HR[e % 2].astype(F32)
+
+    def spread(src, dst, ss, rs, start):
+        def step(d, _):
+            t = lax.rem(me + d, n)
+            c = pltpu.make_async_remote_copy(
+                src(t), dst.at[me], ss.at[t], rs.at[me], device_id={"seq": t}, device_id_type=MESH
+            )
+            c.start()
+            return 0
+
+        def finish(d, _):
+            t = lax.rem(me + d, n)
+            c = pltpu.make_async_remote_copy(
+                src(t), dst.at[t], ss.at[t], rs.at[t], device_id={"seq": t}, device_id_type=MESH
+            )
+            c.wait_recv()
+            c.wait_send()
+            return 0
+
+        lax.fori_loop(1, n, step if start else finish, 0)
+
+    def to_owner(u, rows, ss, rs):
+        c = pltpu.make_async_remote_copy(
+            XM.at[u, pl.ds(0, rows)], OB.at[me, pl.ds(0, rows)], ss.at[u], rs.at[me],
+            device_id={"seq": first_owner + u}, device_id_type=MESH,
+        )
+
+        @pl.when(me != first_owner + u)
+        def _():
+            c.start()
+
+        @pl.when(me == first_owner + u)
+        def _():
+            OB[me, 0:rows] = XM[u, 0:rows]
+
+    def to_owner_sent(u, rows, ss, rs):
+        @pl.when(me != first_owner + u)
+        def _():
+            pltpu.make_async_remote_copy(
+                XM.at[u, pl.ds(0, rows)], OB.at[me, pl.ds(0, rows)], ss.at[u], rs.at[me],
+                device_id={"seq": first_owner + u}, device_id_type=MESH,
+            ).wait_send()
+
+    def owner_gets(rows, ss, rs):
+        def step(d, _):
+            t = lax.rem(me + d, n)
+            pltpu.make_async_remote_copy(
+                XM.at[0, pl.ds(0, rows)], OB.at[t, pl.ds(0, rows)], ss.at[0], rs.at[t],
+                device_id={"seq": t}, device_id_type=MESH,
+            ).wait_recv()
+            return 0
+
+        lax.fori_loop(1, n, step, 0)
+
+    def from_owner(slots, ss, rs, start):
+        def step(d, _):
+            t = lax.rem(me + d, n)
+            c = pltpu.make_async_remote_copy(
+                slots.at[mine], slots.at[mine], ss.at[t], rs.at[mine],
+                device_id={"seq": t}, device_id_type=MESH,
+            )
+            if start:
+                c.start()
+            else:
+                c.wait_send()
+            return 0
+
+        lax.fori_loop(1, n, step, 0)
+
+    def owner_came(slots, u, ss, rs):
+        @pl.when(me != first_owner + u)
+        def _():
+            pltpu.make_async_remote_copy(
+                slots.at[u], slots.at[u], ss.at[0], rs.at[u],
+                device_id={"seq": first_owner + u}, device_id_type=MESH,
+            ).wait_recv()
+
+    def edges(buf, ss, rs, act):
+        after = pltpu.make_async_remote_copy(
+            buf.at[:, pl.ds(L, margin)], buf.at[:, pl.ds(0, margin)], ss.at[0], rs.at[0],
+            device_id={"seq": lax.rem(me + 1, n)}, device_id_type=MESH,
+        )
+        before = pltpu.make_async_remote_copy(
+            buf.at[:, pl.ds(margin, margin)], buf.at[:, pl.ds(margin + L, margin)], ss.at[1], rs.at[1],
+            device_id={"seq": lax.rem(me + n - 1, n)}, device_id_type=MESH,
+        )
+        if act == "start":
+            @pl.when(me < n - 1)
+            def _():
+                after.start()
+
+            @pl.when(me > 0)
+            def _():
+                before.start()
+        else:
+            @pl.when(me < n - 1)
+            def _():
+                after.wait_send()
+                before.wait_recv()
+
+            @pl.when(me > 0)
+            def _():
+                before.wait_send()
+                after.wait_recv()
+
+    def edge_zeros(buf):
+        none = jnp.zeros((B, margin, C), BF16)
+        buf[:, 2 * margin + L :, :] = jnp.zeros((B, 256 - L - 2 * margin, C), BF16)
+
+        @pl.when(me == 0)
+        def _():
+            buf[:, 0:margin, :] = none
+
+        @pl.when(me == n - 1)
+        def _():
+            buf[:, margin + L : 2 * margin + L, :] = none
+
+    def conv(bands, buf, u):
+        b, j = unit(u)
+        x = buf[b, :, j * 128 : (j + 1) * 128]
+        return jnp.where(low_lane, nn(bands[2 * j], x), nn(bands[2 * j + 1], x))
+
+    own_bits = [lax.rem(me // (1 << k), 2) for k in range(NB)]
+    orders = [
+        list(range(NB)),
+        [1, 0] + list(range(2, NB)),
+    ]
+    HALF = G.shape[-1] // 2
+    FH = F // 2
+    items = {
+        "outer0": (0, FH, 0), "inner0": (FH, FH, 0),
+        "tail0": (2 * FH, HALF - 2 * FH, 0),
+        "outer1": (HALF, FH, 1), "inner1": (HALF + FH, FH, 1),
+        "tail1": (HALF + 2 * FH, HALF - 2 * FH, 1),
+    }
+    item_index = {name: i for i, name in enumerate(items)}
+
+    def kept(name, stage):
+        order = orders[items[name][2]]
+        index = [slice(None)] * NB
+        for k in order[:stage]:
+            index[NB - 1 - k] = own_bits[k]
+        return index
+
+    def ref_at(ref, index, cols):
+        full = tuple(pl.ds(0, ref.shape[i]) if isinstance(v, slice) else v for i, v in enumerate(index))
+        return ref.at[full + (pl.ds(0, CH), pl.ds(cols[0], cols[1]))]
+
+    def rs_copy(l, name, stage):
+        first, count, order_id = items[name]
+        k = orders[order_id][stage]
+        index = kept(name, stage)
+        index[NB - 1 - k] = 1 - own_bits[k]
+        src = ref_at(G, index, (first, count))
+        buf = RV[stage]
+        lead = (min(l, buf.shape[0] - 1),)
+        free = NB - 1 - stage
+        dst = buf.at[lead + (pl.ds(0, 2),) * free + (pl.ds(0, CH), pl.ds(first, count))]
+        peer = me + (1 - 2 * own_bits[k]) * (1 << k)
+        i = item_index[name]
+        return pltpu.make_async_remote_copy(
+            src, dst, gsem_s.at[l, i, stage], gsem_r.at[l, i, stage],
+            device_id={"seq": peer}, device_id_type=MESH,
+        )
+
+    def rs_start(l, name, stage):
+        rs_copy(l, name, stage).start()
+
+    def rs_add(l, name, stage):
+        first, count, order_id = items[name]
+        rs_copy(l, name, stage).wait()
+        index = kept(name, stage + 1)
+        buf = RV[stage]
+        lead = min(l, buf.shape[0] - 1)
+        free = [i for i, v in enumerate(index) if isinstance(v, slice)]
+        cols = slice(first, first + count)
+        if free:
+            for code in range(1 << len(free)):
+                spot = [(code >> (len(free) - 1 - i)) & 1 for i in range(len(free))]
+                at = list(index)
+                for f, v in zip(free, spot):
+                    at[f] = v
+                at = tuple(at)
+                G[at + (slice(None), cols)] = (
+                    G[at + (slice(None), cols)].astype(F32)
+                    + buf[(lead,) + tuple(spot) + (slice(None), cols)].astype(F32)
+                ).astype(BF16)
+        else:
+            at = tuple(index)
+            for piece, (c0, cn, put) in outs_of(name, first, count):
+                a = G[at + (slice(None), slice(c0, c0 + cn))].astype(F32)
+                put(l, a + buf[lead, :, c0 : c0 + cn].astype(F32))
+
+    def outs_of(name, first, count):
+        def at(ref, *lead):
+            def put(l, x, c):
+                ref[(l,) + lead + (slice(None), c)] = x
+
+            return put
+
+        def bind(put, c):
+            return lambda l, x: put(l, x, c)
+
+        if name.startswith("outer"):
+            o = 0 if name.endswith("0") else FH
+            return [(0, (first, FH, bind(at(gouter), slice(o, o + FH))))]
+        if name.startswith("inner"):
+            o = 0 if name.endswith("0") else FH
+            return [(0, (first, FH, bind(at(ginner), slice(o, o + FH))))]
+        if name == "tail0":
+            return [
+                (0, (first, 128, bind(at(gout), slice(0, 128)))),
+                (0, (first + 128, C, bind(at(gproj, 0), slice(0, C)))),
+                (0, (first + 128 + C, 256, bind(at(gproj, 2), slice(0, 256)))),
+            ]
+        return [
+            (0, (first, C - 128, bind(at(gout), slice(128, C)))),
+            (0, (first + C - 128, C, bind(at(gproj, 1), slice(0, C)))),
+            (0, (first + 2 * C - 128, C - 256, bind(at(gproj, 2), slice(256, C)))),
+        ]
+
+    def weight_grad(left_t, right, first, count, width):
+        def step(i, _):
+            o = pl.multiple_of(i * width, width)
+            x = nn(left_t, right(o)).astype(BF16)
+            o = pl.multiple_of(first + o, 128)
+            for c in range(n):
+                spot = tuple((c >> (NB - 1 - i)) & 1 for i in range(NB))
+                G[spot + (slice(None), pl.ds(o, width))] = x[c * CH : (c + 1) * CH]
+            return 0
+
+        lax.fori_loop(0, count // width, step, 0)
+
+    HID[...] = tok[...].astype(F32)
+    for l in range(z.layers):
+        for h in range(z.local_heads):
+            for which, store in ((0, TT), (1, TR)):
+                base = jnp.broadcast_to(taps[l, which, h : h + 1, :], (128, 256))
+                store[l, h] = pltpu.roll(base, 0, 1, stride=1, stride_axis=0).astype(BF16)
+
+    def forward(l):
+        copies = weight_copies(l)
+        e = 2 * l
+        hl = HID[...].astype(BF16)
+        HL[l] = hl
+        copies[0].wait()
+        bias_q, bias_v = vec[l, 0:1, 0:C], vec[l, 0:1, C : 2 * C]
+        q = (nn(hl, WP[l, 0]) + bias_q) * scale
+        k = nn(hl, WP[l, 1]) * scale
+        QS[l, 0], QS[l, 1] = halves(q)
+        KS[l, 0], KS[l, 1] = halves(k)
+        for b in range(B):
+            for r in range(S):
+                at = b * L + r * z.segment
+                i = b * S + r
+                MS[i : i + 1, :] = jnp.sum(q[at : at + z.segment], axis=0, keepdims=True) * (1.0 / z.segment)
+                MS[8 + i : 9 + i, :] = jnp.sum(k[at : at + z.segment], axis=0, keepdims=True) * (1.0 / z.segment)
+        spread(lambda t: MS, MB, msem_s.at[l], msem_r.at[l], True)
+        MB[me] = MS[...]
+        vl = (nn(hl, WP[l, 2]) + bias_v).astype(BF16)
+        for b in range(B):
+            VX[l, b, margin : margin + L, :] = vl[b * L : (b + 1) * L]
+        edge_zeros(VX.at[l])
+        edges(VX.at[l], vsem_s.at[l], vsem_r.at[l], "start")
+        spread(lambda t: MS, MB, msem_s.at[l], msem_r.at[l], False)
+        for u in range(U):
+            b, j = unit(u)
+            for i in range(n):
+                at = slice(i * S, (i + 1) * S)
+                QM[l, u, at, :] = MB[i, b * S : (b + 1) * S, j * 128 : (j + 1) * 128]
+                KM[l, u, at, :] = MB[i, 8 + b * S : 8 + (b + 1) * S, j * 128 : (j + 1) * 128]
+        for u in range(U):
+            b, j = unit(u)
+            qb = expand(QM[l, u])
+            ksc = nt3(halves(qb), pair_tile(KS, l, u))
+            KSC[l, u] = ksc
+            top = jnp.max(ksc, axis=1, keepdims=True)
+            p = jnp.exp(ksc - top)
+            total = jnp.sum(p, axis=1, keepdims=True)
+            v = VX[l, b, margin : margin + L, j * 128 : (j + 1) * 128]
+            ph = halves(p)
+            x = nn(jnp.concatenate(ph, axis=1), jnp.concatenate([v, v], axis=0))
+            XM[u, 0:64] = compress(x)
+            XM[u, 64:65] = to_row(top)
+            XM[u, 65:66] = to_row(total)
+            to_owner(u, 72, xsem_s.at[l], xsem_r.at[l])
+        for u in range(U):
+            kb = expand(KM[l, u])
+            s = nt3(pair_tile(QS, l, u), halves(kb))
+            p = jnp.exp(s - half_tops(s))
+            RW[l, u] = p / half_sums(p)
+
+        @pl.when(is_owner)
+        def _():
+            qb, kb = expand(QM[l, mine]), expand(KM[l, mine])
+            s = jnp.where(same_head, nt3f(qb, kb), -jnp.inf)
+            p = jnp.exp(s - jnp.max(s, axis=1, keepdims=True))
+            a = p / jnp.sum(p, axis=1, keepdims=True)
+            PA[l] = a
+            ah = halves(a)
+            sums = jnp.sum(a, axis=0, keepdims=True)
+            tops = jnp.where(
+                low_lane[0:1],
+                jnp.max(jnp.where(low_lane[0:1], sums, 0.0), axis=1, keepdims=True),
+                jnp.max(jnp.where(low_lane[0:1], 0.0, sums), axis=1, keepdims=True),
+            )
+            unit_matrix = jnp.where(eye, 1.0, 0.0)
+
+            def iterate(i, zk):
+                PV[l, i, 0] = zk
+                zh = halves(zk)
+                pr = nn3(ah, zh)
+                PV[l, i, 1] = pr
+                prh = halves(pr)
+                n2 = 15.0 * unit_matrix - nn3(prh, halves(7.0 * unit_matrix - pr))
+                PV[l, i, 2] = n2
+                n3 = 13.0 * unit_matrix - nn3(prh, halves(n2))
+                PV[l, i, 3] = n3
+                return 0.25 * nn3(zh, halves(n3))
+
+            zk = lax.fori_loop(0, PINV_ITERS, iterate, a.T / tops)
+            PZ[l] = zk
+            owner_gets(72, xsem_s.at[l], xsem_r.at[l])
+            tops = OB[0, 64:65]
+            for i in range(1, n):
+                tops = jnp.maximum(tops, OB[i, 64:65])
+            factors = [jnp.exp(OB[i, 64:65] - tops) for i in range(n)]
+            total = factors[0] * OB[0, 65:66]
+            for i in range(1, n):
+                total = total + factors[i] * OB[i, 65:66]
+            mixed = jnp.zeros((64, 128), F32)
+            for i in range(n):
+                col = to_col(factors[i] / total)
+                mixed = mixed + jnp.where(low_lane64, col[0:64], col[64:128]) * OB[i, 0:64]
+            MX[l] = mixed
+            CR[l, mine, 0:64] = compress(nn3f(zk, expand(mixed)))
+            CR[l, mine, 64:65] = tops + jnp.log(total)
+            from_owner(CR.at[l], csem_s.at[l], csem_r.at[l], True)
+
+        edges(VX.at[l], vsem_s.at[l], vsem_r.at[l], "wait")
+        for u in range(U):
+            b, j = unit(u)
+            DQ[b * L : (b + 1) * L, j * 128 : (j + 1) * 128] = conv(TT.at[l], VX.at[l], u)
+        for u in range(U):
+            b, j = unit(u)
+            to_owner_sent(u, 72, xsem_s.at[l], xsem_r.at[l])
+            owner_came(CR.at[l], u, csem_s.at[l], csem_r.at[l])
+            at = (slice(b * L, (b + 1) * L), slice(j * 128, (j + 1) * 128))
+            context = nn3f(RW[l, u], expand(CR[l, u, 0:64])) + DQ[at]
+            CTX[(l,) + at] = context.astype(BF16)
+
+        @pl.when(is_owner)
+        def _():
+            from_owner(CR.at[l], csem_s.at[l], csem_r.at[l], False)
+
+        copies[1].wait()
+        HS[e % 2] = nn(CTX[l], WO[l]).astype(BF16)
+        c = swap(e)
+        c.start()
+        c.wait()
+        total1 = HID[...] + both(e) + vec[l, 2:3, 0:D]
+        T1[l] = total1
+        normed = moments(total1)[0] * vec[l, 4:5, 0:D] + vec[l, 6:7, 0:D]
+        HID[...] = normed
+        NL[l] = normed.astype(BF16)
+        copies[2].wait()
+
+        def grow(i, _):
+            o = pl.ds(pl.multiple_of(i * 256, 256), 256)
+            pre = nn(NL[l], WI[l, :, o]) + vec[l, 1:2, o]
+            below = 0.5 * (1.0 + lax.erf(pre * (0.5**0.5)))
+            ACT[l, :, o] = (pre * below).astype(BF16)
+            GP[l, :, o] = (below + pre * jnp.exp(-0.5 * pre * pre) * 0.3989422804014327).astype(BF16)
+            return 0
+
+        lax.fori_loop(0, F // 256, grow, 0)
+        copies[3].wait()
+
+        def shrink(i, _):
+            o = pl.ds(pl.multiple_of(i * 256, 256), 256)
+            HS[(e + 1) % 2, :, o] = nn(ACT[l], WF[l, :, o]).astype(BF16)
+            return 0
+
+        lax.fori_loop(0, D // 256, shrink, 0)
+        c = swap(e + 1)
+        c.start()
+        c.wait()
+        total2 = HID[...] + both(e + 1) + vec[l, 3:4, 0:D]
+        T2[l] = total2
+        HID[...] = moments(total2)[0] * vec[l, 5:6, 0:D] + vec[l, 7:8, 0:D]
+
+    def backward(l, left):
+        e = 2 * z.layers + 2 * (z.layers - 1 - l)
+        base = 60 * l
+        total2, sums = norm_back(T2[l], UP[...], vec[l, 5:6, 0:D])
+        put_small(base + 6, sums[0])
+        put_small(base + 18, sums[1])
+        put_small(base + 30, sums[2])
+        DT[...] = total2
+        FL[...] = total2.astype(BF16)
+
+        def widen(i, _):
+            o = pl.ds(pl.multiple_of(i * 256, 256), 256)
+            grad = nt(FL[...], WF[l, o, :]).astype(BF16).astype(F32)
+            pre = (GP[l, :, o].astype(F32) * grad).astype(BF16)
+            DPRE[:, o] = pre
+            s = jnp.sum(pre.astype(F32), axis=0, keepdims=True)
+            SM[pl.ds(base + 36 + 2 * i, 1), :] = s[:, 0:128]
+            SM[pl.ds(base + 37 + 2 * i, 1), :] = s[:, 128:256]
+            return 0
+
+        lax.fori_loop(0, F // 256, widen, 0)
+
+        def narrow(i, _):
+            o = pl.ds(pl.multiple_of(i * 256, 256), 256)
+            HS[e % 2, :, o] = nt(DPRE[...], WI[l, o, :]).astype(BF16)
+            return 0
+
+        lax.fori_loop(0, D // 256, narrow, 0)
+        c = swap(e)
+        c.start()
+        for done in left[:1]:
+            done()
+        feed_t = FL[...].T
+        norm_t = NL[l].T
+        for h in range(2):
+            name = f"outer{h}"
+            weight_grad(feed_t, lambda o: ACT[l, :, pl.ds(h * FH + o, 256)], items[name][0], FH, 256)
+            rs_start(l, name, 0)
+        for h in range(2):
+            name = f"inner{h}"
+            weight_grad(norm_t, lambda o: DPRE[:, pl.ds(h * FH + o, 256)], items[name][0], FH, 256)
+            rs_start(l, name, 0)
+        c.wait()
+        grad_normed = DT[...] + both(e)
+        total1, sums = norm_back(T1[l], grad_normed, vec[l, 4:5, 0:D])
+        put_small(base + 0, sums[0])
+        put_small(base + 12, sums[1])
+        put_small(base + 24, sums[2])
+        DT[...] = total1
+        attend = total1.astype(BF16)
+        FL[...] = attend
+        grads = nt(attend, WO[l]).astype(BF16)
+        for b in range(B):
+            GX[b, margin : margin + L, :] = grads[b * L : (b + 1) * L]
+        edge_zeros(GX)
+        edges(GX, vsem_s.at[z.layers + l], vsem_r.at[z.layers + l], "start")
+
+        def g_tile(u):
+            b, j = unit(u)
+            return GX[b, margin : margin + L, j * 128 : (j + 1) * 128]
+
+        for u in range(U):
+            g = g_tile(u)
+            x = tn(jnp.concatenate(halves(RW[l, u]), axis=0), jnp.concatenate([g, g], axis=0))
+            XM[u, 0:64] = compress(x)
+            to_owner(u, 64, xsem_s.at[z.layers + l], xsem_r.at[z.layers + l])
+            DQM[u] = jnp.zeros((64, 128), F32)
+        for u in range(U):
+            b, j = unit(u)
+            at = (slice(b * L, (b + 1) * L), slice(j * 128, (j + 1) * 128))
+            g = g_tile(u)
+            core_pair = halves(expand(CR[l, u, 0:64]))
+            d_row = nt(jnp.concatenate([g, g], axis=1), jnp.concatenate(core_pair, axis=1))
+            rw = RW[l, u]
+            d_rs = halves(rw * (d_row - half_sums(rw * d_row)))
+            DQ[at] = nn3(d_rs, halves(expand(KM[l, u])))
+            DKM[u] = compress(tn3(d_rs, pair_tile(QS, l, u)))
+
+        for done in left[1:2]:
+            done()
+        advance(l, ("outer0", "outer1"), 0)
+
+        @pl.when(is_owner)
+        def _():
+            owner_gets(64, xsem_s.at[z.layers + l], xsem_r.at[z.layers + l])
+            d_core = OB[0, 0:64]
+            for i in range(1, n):
+                d_core = d_core + OB[i, 0:64]
+            PC[...] = d_core
+            d_mixed = tn3f(PZ[l], expand(d_core))
+            DR[mine, 0:64] = compress(d_mixed)
+            DR[mine, 64:65] = to_row(jnp.sum(d_mixed * expand(MX[l]), axis=1, keepdims=True))
+            from_owner(DR, csem_s.at[z.layers + l], csem_r.at[z.layers + l], True)
+
+        for u in range(U):
+            to_owner_sent(u, 64, xsem_s.at[z.layers + l], xsem_r.at[z.layers + l])
+
+        @pl.when(is_owner)
+        def _():
+            a = PA[l]
+            ah = halves(a)
+            unit_matrix = jnp.where(eye, 1.0, 0.0)
+
+            def back(i, carry):
+                dz, da = carry
+                i = PINV_ITERS - 1 - i
+                zh, prh = halves(PV[l, i, 0]), halves(PV[l, i, 1])
+                n1h = halves(7.0 * unit_matrix - PV[l, i, 1])
+                n2h, n3h = halves(PV[l, i, 2]), halves(PV[l, i, 3])
+                dzh = halves(dz)
+                dn3 = halves(0.25 * tn3(zh, dzh))
+                dn2 = halves(-tn3(prh, dn3))
+                dpr = tn3(prh, dn2) - nt3(dn3, n2h) - nt3(dn2, n1h)
+                dpr = halves(dpr)
+                dz = 0.25 * nt3(dzh, n3h) + tn3(ah, dpr)
+                return dz, da + nt3(dpr, zh)
+
+            dz, da = lax.fori_loop(
+                0, PINV_ITERS, back, (nt3f(expand(PC[...]), expand(MX[l])), jnp.zeros((128, 128), F32))
+            )
+            low_row = low_lane[0:1]
+
+            def half_row(x, f):
+                return jnp.where(
+                    low_row,
+                    f(jnp.where(low_row, x, 0.0), axis=1, keepdims=True),
+                    f(jnp.where(low_row, 0.0, x), axis=1, keepdims=True),
+                )
+
+            sums = jnp.sum(a, axis=0, keepdims=True)
+            tops = half_row(sums, jnp.max)
+            d_tops = -half_row(jnp.sum(dz * PV[l, 0, 0], axis=0, keepdims=True), jnp.sum) / tops
+            at_top = jnp.where(sums == tops, 1.0, 0.0)
+            da = da + (dz / tops).T + at_top * d_tops / half_row(at_top, jnp.sum)
+            d_ms = halves(a * (da - jnp.sum(a * da, axis=1, keepdims=True)))
+            DQM[mine] = compress(nn3(d_ms, halves(expand(KM[l, mine]))))
+            DKM[mine] = DKM[mine] + compress(tn3(d_ms, halves(expand(QM[l, mine]))))
+
+        advance(l, ("inner0", "inner1"), 0)
+        advance(l, ("outer0", "outer1"), 1)
+        edges(GX, vsem_s.at[z.layers + l], vsem_r.at[z.layers + l], "wait")
+        for u in range(U):
+            b, j = unit(u)
+            at = (slice(b * L, (b + 1) * L), slice(j * 128, (j + 1) * 128))
+            DV[at] = conv(TR.at[l], GX, u)
+        for j in range(NP):
+            for h in range(2):
+                found = jnp.zeros((128, 256), F32)
+                for b in range(B):
+                    g = nn(flip, g_tile(b * NP + j))
+                    g = jnp.where(low_lane, g, 0.0) if h == 0 else jnp.where(low_lane, 0.0, g)
+                    found = found + nt(g.astype(BF16), VX[l, b, :, j * 128 : (j + 1) * 128])
+                found = pltpu.roll(found, 129, 1, stride=1, stride_axis=0)
+                row = base + 54 + 2 * j + h
+                SM[row : row + 1, :] = jnp.sum(found[:, 0:128], axis=0, keepdims=True)
+        for u in range(U):
+            b, j = unit(u)
+            at = (slice(b * L, (b + 1) * L), slice(j * 128, (j + 1) * 128))
+            owner_came(DR, u, csem_s.at[z.layers + l], csem_r.at[z.layers + l])
+            qbh = halves(expand(QM[l, u]))
+            dmh = halves(expand(DR[u, 0:64]))
+            off = to_col(DR[u, 64:65])
+            kw = jnp.exp(KSC[l, u] - to_col(CR[l, u, 64:65]))
+            v = VX[l, b, margin : margin + L, j * 128 : (j + 1) * 128]
+            DV[at] = DV[at] + tn3(halves(kw), dmh)
+            d_kw = nt(jnp.concatenate(dmh, axis=1), jnp.concatenate([v, v], axis=1))
+            d_ks = halves(kw * (d_kw - off))
+            DK[at] = tn3(d_ks, qbh)
+            DQM[u] = DQM[u] + compress(nn3(d_ks, pair_tile(KS, l, u)))
+
+        @pl.when(is_owner)
+        def _():
+            from_owner(DR, csem_s.at[z.layers + l], csem_r.at[z.layers + l], False)
+
+        advance(l, ("inner0", "inner1"), 1)
+        for done in left[2:3]:
+            done()
+        for u in range(U):
+            b, j = unit(u)
+            lanes = slice(j * 128, (j + 1) * 128)
+            for i in range(n):
+                SB[i, b * S : (b + 1) * S, lanes] = DQM[u, i * S : (i + 1) * S]
+                SB[i, 8 + b * S : 8 + (b + 1) * S, lanes] = DKM[u, i * S : (i + 1) * S]
+        spread(lambda t: SB.at[t], SR, qsem_s.at[l], qsem_r.at[l], True)
+        SR[me] = SB[me]
+        advance(l, ("outer0", "outer1"), 2)
+        for done in left[3:]:
+            done()
+        spread(lambda t: SB.at[t], SR, qsem_s.at[l], qsem_r.at[l], False)
+        marks = SR[0]
+        for i in range(1, n):
+            marks = marks + SR[i]
+        marks = marks * (1.0 / z.segment)
+        for b in range(B):
+            for r in range(S):
+                at = slice(b * L + r * z.segment, b * L + (r + 1) * z.segment)
+                i = b * S + r
+                DP[at, 0:C] = ((DQ[at] + marks[i : i + 1]) * scale).astype(BF16)
+                DP[at, C : 2 * C] = ((DK[at] + marks[8 + i : 9 + i]) * scale).astype(BF16)
+        DP[:, 2 * C : 3 * C] = DV[...].astype(BF16)
+
+        def onto(i, _):
+            o = pl.ds(pl.multiple_of(i * 256, 256), 256)
+            x = nt(DP[:, 0:C], WP[l, 0, o, :]) + nt(DP[:, C : 2 * C], WP[l, 1, o, :])
+            HS[(e + 1) % 2, :, o] = (x + nt(DP[:, 2 * C : 3 * C], WP[l, 2, o, :])).astype(BF16)
+            return 0
+
+        lax.fori_loop(0, D // 256, onto, 0)
+        c = swap(e + 1)
+        c.start()
+        bias = jnp.sum(DP[...].astype(F32), axis=0, keepdims=True)
+        put_small(base + 48, bias[:, 0:C])
+        put_small(base + 51, bias[:, 2 * C : 3 * C])
+        attend_t = FL[...].T
+        hidden_t = HL[l].T
+        t0, t1 = items["tail0"][0], items["tail1"][0]
+        weight_grad(attend_t, lambda o: CTX[l, :, pl.ds(o, 128)], t0, 128, 128)
+        weight_grad(hidden_t, lambda o: DP[:, pl.ds(o, 128)], t0 + 128, C, 128)
+        weight_grad(hidden_t, lambda o: DP[:, pl.ds(2 * C + o, 256)], t0 + 128 + C, 256, 256)
+        rs_start(l, "tail0", 0)
+        weight_grad(attend_t, lambda o: CTX[l, :, pl.ds(128 + o, 256)], t1, C - 128, 256)
+        weight_grad(hidden_t, lambda o: DP[:, pl.ds(C + o, 128)], t1 + C - 128, C, 128)
+        weight_grad(hidden_t, lambda o: DP[:, pl.ds(2 * C + 256 + o, 128)], t1 + 2 * C - 128, C - 256, 128)
+        rs_start(l, "tail1", 0)
+        c.wait()
+        UP[...] = DT[...] + both(e + 1)
+        advance(l, ("inner0", "inner1"), 2)
+        advance(l, ("outer0", "outer1"), 3)
+
+    def advance(l, names, stage):
+        for name in names:
+            rs_add(l, name, stage)
+            if stage + 1 < NB:
+                rs_start(l, name, stage + 1)
+
+    for l in range(z.layers):
+        forward(l)
+    result[...] = HID[...]
+    pltpu.make_async_copy(ups, UP, wsem.at[0, 4]).wait()
+    left = []
+    for l in range(z.layers - 1, -1, -1):
+        backward(l, left)
+        left = [
+            partial(advance, l, ("inner0", "inner1"), 3),
+        ] + [partial(advance, l, ("tail0", "tail1"), s) for s in range(NB)]
+    gtok[...] = UP[...]
+    spread(lambda t: SM.at[pl.ds(pl.multiple_of(t * 8, 8), 8)], SMR, ssem_s, ssem_r, True)
+    SMR[me] = SM[pl.ds(pl.multiple_of(me * 8, 8), 8), :]
+    left[0]()
+    left[1]()
+    spread(lambda t: SM.at[pl.ds(pl.multiple_of(t * 8, 8), 8)], SMR, ssem_s, ssem_r, False)
+    total = SMR[0]
+    for i in range(1, n):
+        total = total + SMR[i]
+    SMT[me] = total
+    spread(lambda t: SMT.at[me], SMT, tsem_s, tsem_r, True)
+    for done in left[2:]:
+        done()
+    spread(lambda t: SMT.at[me], SMT, tsem_s, tsem_r, False)
+    for i in range(n):
+        gsmall[i * 8 : (i + 1) * 8, :] = SMT[i]
+
+
+def fused(z, tokens, cotangent, masked, projections, projection_bias, conv_taps, output_weight,
+          output_bias, norm_gain, norm_shift, inner_weight, inner_bias, outer_weight):
+    n, B, L, R, D, C, F = z.n, z.batch, z.length, z.rows, z.width, z.cols, z.hidden
+    U, H, NL_, NB, CH = z.units, z.local_heads, z.layers, z.bits, z.width // z.n
+    wide = max(F, 2 * C, D)
+
+    def padded(x):
+        return jnp.pad(x.astype(F32), [(0, 0)] * (x.ndim - 1) + [(0, wide - x.shape[-1])])
+
+    vec = jnp.concatenate(
+        [
+            padded(projection_bias.reshape(NL_, 1, 2 * C)),
+            padded(inner_bias[:, None]),
+            padded(output_bias),
+            padded(norm_gain),
+            padded(norm_shift),
+        ],
+        axis=1,
+    )
+    taps = jnp.stack([conv_taps, conv_taps[:, :, ::-1]], axis=1).astype(F32)
+    taps = jnp.pad(taps, ((0, 0), (0, 0), (0, 8 - H), (0, 256 - z.kernel)))
+    ups = (cotangent.astype(F32) * masked.astype(F32)[:, :, None]).reshape(R, D)
+    V = pltpu.VMEM
+    DMA = pltpu.SemaphoreType.DMA
+    cols = 2 * F + 4 * C
+    scratch = dict(
+        WP=V((NL_, 3, D, C), BF16), WO=V((NL_, C, D), BF16), WI=V((NL_, D, F), BF16), WF=V((NL_, F, D), BF16),
+        HL=V((NL_, R, D), BF16), QS=V((NL_, 2, R, C), BF16), KS=V((NL_, 2, R, C), BF16),
+        VX=V((NL_, B, 256, C), BF16), RW=V((NL_, U, 128, 128), F32), KSC=V((NL_, U, 128, 128), F32),
+        CTX=V((NL_, R, C), BF16), T1=V((NL_, R, D), F32), T2=V((NL_, R, D), F32), NL=V((NL_, R, D), BF16),
+        GP=V((NL_, R, F), BF16), ACT=V((NL_, R, F), BF16),
+        QM=V((NL_, U, 64, 128), F32), KM=V((NL_, U, 64, 128), F32), CR=V((NL_, U, 72, 128), F32),
+        MX=V((NL_, 64, 128), F32), PA=V((NL_, 128, 128), F32), PV=V((NL_, PINV_ITERS, 4, 128, 128), F32),
+        PZ=V((NL_, 128, 128), F32), PC=V((64, 128), F32),
+        HID=V((R, D), F32), UP=V((R, D), F32), DT=V((R, D), F32), FL=V((R, D), BF16), DPRE=V((R, F), BF16),
+        GX=V((B, 256, C), BF16), DQ=V((R, C), F32), DK=V((R, C), F32), DV=V((R, C), F32), DP=V((R, 3 * C), BF16),
+        DQM=V((U, 64, 128), F32), DKM=V((U, 64, 128), F32), DR=V((U, 72, 128), F32), SM=V((n * 8, 128), F32),
+        TT=V((NL_, H, 128, 256), BF16), TR=V((NL_, H, 128, 256), BF16),
+        MS=V((16, C), F32), MB=V((n, 16, C), F32), XM=V((U, 72, 128), F32), OB=V((n, 72, 128), F32),
+        SB=V((n, 16, C), F32), SR=V((n, 16, C), F32), HS=V((2, R, D), BF16), HR=V((2, R, D), BF16),
+        SMR=V((n, 8, 128), F32), SMT=V((n, 8, 128), F32),
+        G=V((2,) * NB + (CH, cols), BF16),
+        RV=[V((1 if s < 2 else NL_,) + (2,) * (NB - 1 - s) + (CH, cols), BF16) for s in range(NB)],
+        wsem=DMA((NL_, 5)),
+        hsem_s=DMA((4 * NL_,)), hsem_r=DMA((4 * NL_,)),
+        msem_s=DMA((NL_, n)), msem_r=DMA((NL_, n)), xsem_s=DMA((2 * NL_, U)), xsem_r=DMA((2 * NL_, n)),
+        csem_s=DMA((2 * NL_, n)), csem_r=DMA((2 * NL_, U)), vsem_s=DMA((2 * NL_, 2)), vsem_r=DMA((2 * NL_, 2)),
+        gsem_s=DMA((NL_, 6, NB)), gsem_r=DMA((NL_, 6, NB)), qsem_s=DMA((NL_, n)), qsem_r=DMA((NL_, n)),
+        ssem_s=DMA((n,)), ssem_r=DMA((n,)), tsem_s=DMA((n,)), tsem_r=DMA((n,)),
+    )
+    in_vmem = pl.BlockSpec(memory_space=pltpu.VMEM)
+    in_hbm = pl.BlockSpec(memory_space=pl.ANY)
+    out = lambda *s: jax.ShapeDtypeStruct(s, F32)
+    outs = pl.pallas_call(
+        partial(fused_kernel, z),
+        out_shape=(
+            out(R, D), out(R, D), out(NL_, 3, CH, C), out(NL_, CH, C), out(NL_, CH, F), out(NL_, CH, F),
+            out(n * 8, 128),
+        ),
+        in_specs=[in_vmem, in_hbm, in_vmem, in_vmem] + [in_hbm] * 4,
+        out_specs=(in_vmem,) * 7,
+        scratch_shapes=scratch,
+        compiler_params=pltpu.CompilerParams(
+            collective_id=1, has_side_effects=True, vmem_limit_bytes=VMEM_LIMIT
+        ),
+    )(tokens.reshape(R, D), ups, vec, taps, projections, output_weight, inner_weight, outer_weight)
+    result, gtok, gproj, gout, ginner, gouter, small = outs
+    small = small[: 60 * NL_].reshape(NL_, 60, 128)
+
+    def pair(at):
+        return small[:, at : at + 2 * (D // 128)].reshape(NL_, 2, D)
+
+    k = D // 128
+    gain, shift, bias = pair(0), pair(2 * k), pair(4 * k)
+    at = 6 * k
+    grad_inner_bias = small[:, at : at + F // 128].reshape(NL_, F)
+    at += F // 128
+    grad_bias = small[:, at : at + 2 * C // 128].reshape(NL_, 2, C)
+    at += 2 * C // 128
+    grad_taps = small[:, at : at + H, : z.kernel]
+    return (
+        result.reshape(B, L, D), gtok.reshape(B, L, D), gproj, grad_bias, grad_taps,
+        jnp.swapaxes(gout, 1, 2), bias, gain, shift, ginner, grad_inner_bias, jnp.swapaxes(gouter, 1, 2),
+    )
+
+
 def solution(mesh):
     in_specs = (
         P(None, "seq", None),
@@ -537,6 +1500,12 @@
         P(None, "head"),
         P(None, "head", "seq"),
     )
-    return jax.shard_map(
-        on_device, mesh=mesh, in_specs=in_specs, out_specs=out_specs, check_vma=False
-    )
+
+    def whole(*args):
+        z = Fast(mesh.shape, args[0], args[5], args[10])
+        body = partial(fused, z) if z.fits() else on_device
+        return jax.shard_map(
+            body, mesh=mesh, in_specs=in_specs, out_specs=out_specs, check_vma=False
+        )(*args)
+
+    return whole

time: 3160 us -> 317 us (0.10); the launches traced: 3120 us -> 317 us
  waiting for transfers between devices: 1740 us -> 0 us
  local copies, waits for them, and re-layouts: 472 us -> 17.2 us
  Pallas kernels: 0 us -> 295 us
  matrix products: 256 us -> 0 us
  loops' own time: 243 us -> 0 us
  other arithmetic: 188 us -> 3.97 us
  blocking collectives: 176 us -> 0 us
    reduce_scatter x14 -> x0, waiting for transfers between devices: 861 us -> none  [the longest x2 283 us: on_device(): lax.psum_scatter(gradients[7], 'seq', scatter_dimension=0, tiled=True)]
    psum x9 -> x0, waiting for transfers between devices: 593 us -> none  [the longest x4 258 us: forward_layer(): lax.psum((jnp.einsum('mt,btc->bmc', selector, query_rows, precision=exact...]
    pallas_call x0 -> x1, Pallas kernels: none -> 295 us  [fused(): pl.pallas_call(partial(fused_kernel, z), out_shape=(out(R, D), out(R, D),...]
    unnamed x25 -> x0, waiting for transfers between devices: 285 us -> none
    dot_general x212 -> x0, matrix products: 256 us -> none  [the longest x72 51.9 us: pseudo_inverse(): jnp.matmul(product, nested, precision=exact_result)]
    another operation x6 -> x0, loops' own time: 243 us -> none  [the longest x2 238 us: tap_sums(): return lax.map(one_tap, jnp.arange(kernel, dtype=jnp.int32))]
    dynamic_slice x393 -> x0, local copies, waits for them, and re-layouts: 222 us -> none  [the longest x260 144 us: add_tap(): lax.dynamic_index_in_dim(broad_kernel_taps, offset, 0, False)]
    dynamic_update_slice x131 -> x0, local copies, waits for them, and re-layouts: 172 us -> none  [the longest x130 172 us: tap_sums(): return lax.map(one_tap, jnp.arange(kernel, dtype=jnp.int32))]
  transfers between devices with their start and end apart: 32 -> 0, of which waited for: 24 -> 0; matrix products, arithmetic and copies ran while one was open for 15% -> 0% of each run, Pallas kernels for 0% -> 0%
where the time goes in v1:
time: 317 us
  Pallas kernels  295 us (93%)
  local copies, waits for them, and re-layouts  17.2 us (5%)
  other arithmetic  3.97 us (1%)
    pallas_call x1, Pallas kernels, fused(): pl.pallas_call(partial(fused_kernel, z), out_shape=(out(R, D), out(R, D),...  295 us
    unnamed x16, local copies, waits for them, and re-layouts  10.1 us

profile of v1, /device:TPU:0, one launch (start us, length us, event | category | flops | bytes accessed | tf_op | source)
XLA Modules:
  0.0 316.6 jit_solution(6338106704359760664)
XLA Ops:
  0.6 0.7 convert_element_type.35
  1.3 0.7 copy.38
  2.1 0.7 convert_element_type.38
  2.8 0.7 pad.25
  3.5 0.7 pad.26
  4.2 0.7 pad.27
  4.9 0.7 copy.29
  5.7 0.6 fusion.6.taps
  6.4 0.6 concatenate.6.vec
  7.0 2.0 convert_multiply_fusion
  9.0 294.7 %shard_map.220 = (f32[256,768]{1,0:T(8,128)}, f32[256,768]{1,0:T(8,128)}, f32[2,3,48,384]{3,2,1,0:T(8,128)}, f32[2,48,384]{2,1,0:T(8,128)}, f32[2,48,1536]{2,1,0...) custom-call(bf16[256,768]{1,0:T(8,128)(2,1)} %bitcast.20, f32[256,768]{1,0:T(8,128)} %bitcast.16, ...), custom_call_target="tpu_custom_call" | custom-call | tf_op jit(solution)/shard_map/pallas_call | solution.py:1440
  303.8 0.9 slice.21
  304.7 0.6 copy.32
  305.3 0.6 reshape.77
  306.0 0.6 copy.37
  306.6 0.6 reshape.80
  307.2 0.6 reshape.79
  307.8 0.6 reshape.78
  308.4 2.1 copy.45
  310.5 2.1 copy.46
  312.5 1.8 copy.47
  314.3 0.7 copy.48
  315.0 0.8 copy.49
  315.8 0.8 copy.50
  (13 shorter events, 0.2 us)
Async XLA Ops:
  303.8 10.6 %copy-start.2 = (f32[2,48,384]{2,1,0:T(8,128)S(1)}, f32[2,48,384]{2,1,0:T(8,128)}, u32[]{:S(2)}) copy-start(f32[2,48,384]{2,1,0:T(8,128)} %get-tuple-element.23) | copy-start | bytes 442372
  303.8 11.2 %copy-start.1 = (f32[2,48,1536]{2,1,0:T(8,128)S(1)}, f32[2,48,1536]{2,1,0:T(8,128)}, u32[]{:S(2)}) copy-start(f32[2,48,1536]{2,1,0:T(8,128)} %get-tuple-element.65) | copy-start | bytes 1769476
  303.8 12.0 %copy-start = (f32[2,48,1536]{2,1,0:T(8,128)S(1)}, f32[2,48,1536]{2,1,0:T(8,128)}, u32[]{:S(2)}) copy-start(f32[2,48,1536]{2,1,0:T(8,128)} %get-tuple-element.25) | copy-start | bytes 1769476

commit v2 on v1

--- a/solution.py
+++ b/solution.py
@@ -604,16 +604,17 @@
 
 def fused_kernel(
     z,
-    tok, ups, vec, taps, wp_hbm, wo_hbm, wi_hbm, wf_hbm,
-    result, gtok, gproj, gout, ginner, gouter, gsmall,
+    tok, cot, mask, pbias, taps, obias, ngain, nshift, ibias, wp_hbm, wo_hbm, wi_hbm, wf_hbm,
+    result, gtok, gproj, gbias, gtaps, gout, gobias, ggain, gshift, ginner, gibias, gouter,
     *,
     WP, WO, WI, WF,
-    HL, QS, KS, VX, RW, KSC, CTX, T1, T2, NL, GP, ACT, QM, KM, CR, MX, PA, PV, PZ, PC,
-    HID, UP, DT, FL, DPRE, GX, DQ, DK, DV, DP, DQM, DKM, DR, SM, TT, TR,
+    QS, KS, VX, RW, KSC, CTX, T1, T2, GP, ACT, QM, KM, CR, MX, PA, PV, PZ, PC, LTH, LTN,
+    HID, UP, LOW, DPRE, GX, DQ, DK, DV, DP, DQM, DKM, DR, SM, TB, TT, TR, LTF, LTA,
+    LSH, LSN,
     MS, MB, XM, OB, SB, SR, HS, HR, SMR, SMT,
     G, RV,
     wsem, hsem_s, hsem_r, msem_s, msem_r, xsem_s, xsem_r, csem_s, csem_r, vsem_s, vsem_r,
-    gsem_s, gsem_r, qsem_s, qsem_r, ssem_s, ssem_r, tsem_s, tsem_r,
+    asem_s, asem_r, gsem_s, gsem_r, qsem_s, qsem_r, ssem_s, ssem_r, tsem_s, tsem_r,
 ):
     n, B, L, R, D, C, F = z.n, z.batch, z.length, z.rows, z.width, z.cols, z.hidden
     U, NP, S, K = z.units, z.local_heads // 2, z.spans, z.kernel
@@ -639,7 +640,6 @@
     for l in range(z.layers):
         for c in weight_copies(l):
             c.start()
-    pltpu.make_async_copy(ups, UP, wsem.at[0, 4]).start()
 
     barrier = pltpu.get_barrier_semaphore()
 
@@ -666,6 +666,9 @@
             [jnp.where(low_lane64, c, 0.0), jnp.where(low_lane64, 0.0, c)], axis=0
         )
 
+    def expand_low(c):
+        return expand(c.astype(F32)).astype(BF16)
+
     def compress(x):
         return jnp.where(low_lane64, x[0:64], x[64:128])
 
@@ -684,6 +687,22 @@
         a = jnp.max(jnp.where(low_lane, x, -jnp.inf), axis=1, keepdims=True)
         b = jnp.max(jnp.where(low_lane, -jnp.inf, x), axis=1, keepdims=True)
         return jnp.where(low_lane, a, b)
+
+    def parts3(x):
+        a = x.astype(BF16)
+        rest = x - a.astype(F32)
+        b = rest.astype(BF16)
+        c = (rest - b.astype(F32)).astype(BF16)
+        return jnp.concatenate([a.astype(F32), b.astype(F32), c.astype(F32)], axis=0)
+
+    def pack(body, rows):
+        tail = jnp.concatenate([parts3(r) for r in rows], axis=0)
+        fill = jnp.zeros((16 - tail.shape[0], 128), F32)
+        return jnp.concatenate([body, tail, fill], axis=0).astype(BF16)
+
+    def packed_row(message, i):
+        x = message[64 + 3 * i : 67 + 3 * i].astype(F32)
+        return jnp.sum(x, axis=0, keepdims=True)
 
     def unit(u):
         return u // NP, u % NP
@@ -852,131 +871,147 @@
         x = buf[b, :, j * 128 : (j + 1) * 128]
         return jnp.where(low_lane, nn(bands[2 * j], x), nn(bands[2 * j + 1], x))
 
+    DT, FL, LSF, LSA = HID, LOW, LSH, LSN
     own_bits = [lax.rem(me // (1 << k), 2) for k in range(NB)]
-    orders = [
-        list(range(NB)),
-        [1, 0] + list(range(2, NB)),
-    ]
-    HALF = G.shape[-1] // 2
+    dims = [[k for k in reversed(range(NB)) if k != g] for g in range(2)]
     FH = F // 2
-    items = {
-        "outer0": (0, FH, 0), "inner0": (FH, FH, 0),
-        "tail0": (2 * FH, HALF - 2 * FH, 0),
-        "outer1": (HALF, FH, 1), "inner1": (HALF + FH, FH, 1),
-        "tail1": (HALF + 2 * FH, HALF - 2 * FH, 1),
-    }
+    HALF = G.shape[-1]
+    everything = pl.ds(0, 2)
+    items = {"outer": (0, FH), "inner": (FH, FH), "outval": (2 * FH, C), "keyed": (2 * FH + C, C)}
     item_index = {name: i for i, name in enumerate(items)}
 
-    def kept(name, stage):
-        order = orders[items[name][2]]
-        index = [slice(None)] * NB
-        for k in order[:stage]:
-            index[NB - 1 - k] = own_bits[k]
-        return index
-
-    def ref_at(ref, index, cols):
-        full = tuple(pl.ds(0, ref.shape[i]) if isinstance(v, slice) else v for i, v in enumerate(index))
-        return ref.at[full + (pl.ds(0, CH), pl.ds(cols[0], cols[1]))]
-
-    def rs_copy(l, name, stage):
-        first, count, order_id = items[name]
-        k = orders[order_id][stage]
-        index = kept(name, stage)
-        index[NB - 1 - k] = 1 - own_bits[k]
-        src = ref_at(G, index, (first, count))
-        buf = RV[stage]
-        lead = (min(l, buf.shape[0] - 1),)
-        free = NB - 1 - stage
-        dst = buf.at[lead + (pl.ds(0, 2),) * free + (pl.ds(0, CH), pl.ds(first, count))]
-        peer = me + (1 - 2 * own_bits[k]) * (1 << k)
+    def peer_of(k):
+        return me + (1 - 2 * own_bits[k]) * (1 << k)
+
+    def pair_copy(l, i, g, src, dst):
+        return pltpu.make_async_remote_copy(
+            src, dst, asem_s.at[l, i, g], asem_r.at[l, i, g],
+            device_id={"seq": peer_of(g)}, device_id_type=MESH,
+        )
+
+    def right_copies(l, i, ref, ranges):
+        return [
+            pair_copy(l, i, g, ref.at[pl.ds(0, R), pl.ds(c0, cn)], ref.at[pl.ds(R, R), pl.ds(c0, cn)])
+            for g, (c0, cn) in enumerate(ranges)
+        ]
+
+    def left_copies(l, i, stage, gathered):
+        got = []
+        for g in range(2):
+            at = [everything] * NB
+            at[NB - 1 - g] = 1 - own_bits[g]
+            src = stage.at[tuple(at) + (pl.ds(0, CH), pl.ds(0, R))]
+            dst = gathered.at[(g,) + (everything,) * (NB - 1) + (pl.ds(0, CH), pl.ds(R, R))]
+            got.append(pair_copy(l, i, g, src, dst))
+        return got
+
+    def left_put(x, stage, gathered):
+        stage[...] = x.T.reshape(stage.shape)
+        for g in range(2):
+            for code in range(n // 2):
+                spot = tuple((code >> (NB - 2 - i)) & 1 for i in range(NB - 1))
+                at = list(spot)
+                at.insert(NB - 1 - g, own_bits[g])
+                gathered[(g,) + spot + (slice(None), slice(0, R))] = stage[tuple(at)]
+
+    def start_all(copies):
+        for c in copies:
+            c.start()
+
+    def wait_all(copies):
+        for c in copies:
+            c.wait()
+
+    def weight_grad(g, left, right, first, count, width):
+        def step(i, _):
+            o = pl.multiple_of(i * width, width)
+            x = nn(left[g].reshape(D // 2, 2 * R), right(o)).astype(BF16)
+            o = pl.multiple_of(first + o, 128)
+            for code in range(n // 2):
+                spot = tuple((code >> (NB - 2 - i)) & 1 for i in range(NB - 1))
+                G[(g,) + spot + (slice(None), pl.ds(o, width))] = x[code * CH : (code + 1) * CH]
+            return 0
+
+        lax.fori_loop(0, count // width, step, 0)
+
+    STAGES = NB - 1
+
+    def rs_copy(l, name, g, stage):
+        first, count = items[name]
+        cols = (pl.ds(0, CH), pl.ds(first, count))
+        d = NB - 2 - stage
+        index = [everything] * d + [1 - own_bits[dims[g][d]]] + [own_bits[k] for k in dims[g][d + 1 :]]
         i = item_index[name]
         return pltpu.make_async_remote_copy(
-            src, dst, gsem_s.at[l, i, stage], gsem_r.at[l, i, stage],
-            device_id={"seq": peer}, device_id_type=MESH,
+            G.at[(g,) + tuple(index) + cols], RV[stage].at[(l, g) + (everything,) * d + cols],
+            gsem_s.at[l, i, g, stage], gsem_r.at[l, i, g, stage],
+            device_id={"seq": peer_of(dims[g][d])}, device_id_type=MESH,
         )
 
     def rs_start(l, name, stage):
-        rs_copy(l, name, stage).start()
+        for g in range(2):
+            rs_copy(l, name, g, stage).start()
 
     def rs_add(l, name, stage):
-        first, count, order_id = items[name]
-        rs_copy(l, name, stage).wait()
-        index = kept(name, stage + 1)
-        buf = RV[stage]
-        lead = min(l, buf.shape[0] - 1)
-        free = [i for i, v in enumerate(index) if isinstance(v, slice)]
-        cols = slice(first, first + count)
-        if free:
-            for code in range(1 << len(free)):
-                spot = [(code >> (len(free) - 1 - i)) & 1 for i in range(len(free))]
-                at = list(index)
-                for f, v in zip(free, spot):
-                    at[f] = v
-                at = tuple(at)
-                G[at + (slice(None), cols)] = (
-                    G[at + (slice(None), cols)].astype(F32)
-                    + buf[(lead,) + tuple(spot) + (slice(None), cols)].astype(F32)
-                ).astype(BF16)
+        first, count = items[name]
+        for g in range(2):
+            rs_copy(l, name, g, stage).wait()
+            d = NB - 2 - stage
+            mine_at = tuple(own_bits[k] for k in dims[g][d:])
+            cols = (slice(None), slice(first, first + count))
+            if d:
+                for code in range(1 << d):
+                    spot = tuple((code >> (d - 1 - i)) & 1 for i in range(d))
+                    at = (g,) + spot + mine_at + cols
+                    G[at] = G[at] + RV[stage][(l, g) + spot + cols]
+            else:
+                x = G[(g,) + mine_at + cols].astype(F32) + RV[stage][(l, g) + cols].astype(F32)
+                write_out(l, name, g, x)
+
+    def write_out(l, name, g, x):
+        if name == "outer":
+            gouter[l, :, g * FH : (g + 1) * FH] = x
+        elif name == "inner":
+            ginner[l, :, g * FH : (g + 1) * FH] = x
+        elif name == "keyed":
+            gproj[l, g] = x
+        elif g == 0:
+            gout[l, :, 0:128] = x[:, 0:128]
+            gproj[l, 2, :, 0 : C - 128] = x[:, 128:C]
         else:
-            at = tuple(index)
-            for piece, (c0, cn, put) in outs_of(name, first, count):
-                a = G[at + (slice(None), slice(c0, c0 + cn))].astype(F32)
-                put(l, a + buf[lead, :, c0 : c0 + cn].astype(F32))
-
-    def outs_of(name, first, count):
-        def at(ref, *lead):
-            def put(l, x, c):
-                ref[(l,) + lead + (slice(None), c)] = x
-
-            return put
-
-        def bind(put, c):
-            return lambda l, x: put(l, x, c)
-
-        if name.startswith("outer"):
-            o = 0 if name.endswith("0") else FH
-            return [(0, (first, FH, bind(at(gouter), slice(o, o + FH))))]
-        if name.startswith("inner"):
-            o = 0 if name.endswith("0") else FH
-            return [(0, (first, FH, bind(at(ginner), slice(o, o + FH))))]
-        if name == "tail0":
-            return [
-                (0, (first, 128, bind(at(gout), slice(0, 128)))),
-                (0, (first + 128, C, bind(at(gproj, 0), slice(0, C)))),
-                (0, (first + 128 + C, 256, bind(at(gproj, 2), slice(0, 256)))),
-            ]
-        return [
-            (0, (first, C - 128, bind(at(gout), slice(128, C)))),
-            (0, (first + C - 128, C, bind(at(gproj, 1), slice(0, C)))),
-            (0, (first + 2 * C - 128, C - 256, bind(at(gproj, 2), slice(256, C)))),
-        ]
-
-    def weight_grad(left_t, right, first, count, width):
-        def step(i, _):
-            o = pl.multiple_of(i * width, width)
-            x = nn(left_t, right(o)).astype(BF16)
-            o = pl.multiple_of(first + o, 128)
-            for c in range(n):
-                spot = tuple((c >> (NB - 1 - i)) & 1 for i in range(NB))
-                G[spot + (slice(None), pl.ds(o, width))] = x[c * CH : (c + 1) * CH]
-            return 0
-
-        lax.fori_loop(0, count // width, step, 0)
-
-    HID[...] = tok[...].astype(F32)
+            gout[l, :, 128:C] = x[:, 0 : C - 128]
+            gproj[l, 2, :, C - 128 : C] = x[:, C - 128 : C]
+
+    def advance(l, name, stage):
+        rs_add(l, name, stage)
+        if stage + 1 < STAGES:
+            rs_start(l, name, stage + 1)
+
+    out_ranges = ((0, 128), (128, C - 128))
+    val_ranges = ((2 * C, C - 128), (3 * C - 128, 128))
+    key_ranges = ((0, C), (C, C))
+    ffn_ranges = ((0, FH), (FH, FH))
+
+    for b in range(B):
+        HID[b * L : (b + 1) * L, :] = tok[b].astype(F32)
+    TB[...] = jnp.zeros_like(TB)
+    backwards = jnp.where(row_id + lane_id == K - 1, 1.0, 0.0).astype(BF16)
     for l in range(z.layers):
+        TB[0, 0 : z.local_heads, 0:K] = taps[l].astype(F32)
+        TB[1, :, 0:128] = nn(TB[0, :, 0:128].astype(BF16), backwards)
         for h in range(z.local_heads):
             for which, store in ((0, TT), (1, TR)):
-                base = jnp.broadcast_to(taps[l, which, h : h + 1, :], (128, 256))
+                base = jnp.broadcast_to(TB[which, h : h + 1, :], (128, 256))
                 store[l, h] = pltpu.roll(base, 0, 1, stride=1, stride_axis=0).astype(BF16)
 
     def forward(l):
         copies = weight_copies(l)
         e = 2 * l
         hl = HID[...].astype(BF16)
-        HL[l] = hl
+        LOW[...] = hl
         copies[0].wait()
-        bias_q, bias_v = vec[l, 0:1, 0:C], vec[l, 0:1, C : 2 * C]
+        both_bias = pbias[l].astype(F32)
+        bias_q, bias_v = both_bias[0:1], both_bias[1:2]
         q = (nn(hl, WP[l, 0]) + bias_q) * scale
         k = nn(hl, WP[l, 1]) * scale
         QS[l, 0], QS[l, 1] = halves(q)
@@ -994,6 +1029,7 @@
             VX[l, b, margin : margin + L, :] = vl[b * L : (b + 1) * L]
         edge_zeros(VX.at[l])
         edges(VX.at[l], vsem_s.at[l], vsem_r.at[l], "start")
+        left_put(LOW[...], LSH, LTH.at[l])
         spread(lambda t: MS, MB, msem_s.at[l], msem_r.at[l], False)
         for u in range(U):
             b, j = unit(u)
@@ -1010,12 +1046,9 @@
             p = jnp.exp(ksc - top)
             total = jnp.sum(p, axis=1, keepdims=True)
             v = VX[l, b, margin : margin + L, j * 128 : (j + 1) * 128]
-            ph = halves(p)
-            x = nn(jnp.concatenate(ph, axis=1), jnp.concatenate([v, v], axis=0))
-            XM[u, 0:64] = compress(x)
-            XM[u, 64:65] = to_row(top)
-            XM[u, 65:66] = to_row(total)
-            to_owner(u, 72, xsem_s.at[l], xsem_r.at[l])
+            XM[u] = pack(compress(nn(p.astype(BF16), v)), [to_row(top), to_row(total)])
+            to_owner(u, 80, xsem_s.at[l], xsem_r.at[l])
+        start_all(left_copies(l, 0, LSH, LTH.at[l]))
         for u in range(U):
             kb = expand(KM[l, u])
             s = nt3(pair_tile(QS, l, u), halves(kb))
@@ -1052,21 +1085,21 @@
 
             zk = lax.fori_loop(0, PINV_ITERS, iterate, a.T / tops)
             PZ[l] = zk
-            owner_gets(72, xsem_s.at[l], xsem_r.at[l])
-            tops = OB[0, 64:65]
+            owner_gets(80, xsem_s.at[l], xsem_r.at[l])
+            tops = [packed_row(OB.at[i], 0) for i in range(n)]
+            top = tops[0]
             for i in range(1, n):
-                tops = jnp.maximum(tops, OB[i, 64:65])
-            factors = [jnp.exp(OB[i, 64:65] - tops) for i in range(n)]
-            total = factors[0] * OB[0, 65:66]
+                top = jnp.maximum(top, tops[i])
+            factors = [jnp.exp(x - top) for x in tops]
+            total = factors[0] * packed_row(OB.at[0], 1)
             for i in range(1, n):
-                total = total + factors[i] * OB[i, 65:66]
+                total = total + factors[i] * packed_row(OB.at[i], 1)
             mixed = jnp.zeros((64, 128), F32)
             for i in range(n):
                 col = to_col(factors[i] / total)
-                mixed = mixed + jnp.where(low_lane64, col[0:64], col[64:128]) * OB[i, 0:64]
+                mixed = mixed + jnp.where(low_lane64, col[0:64], col[64:128]) * OB[i, 0:64].astype(F32)
             MX[l] = mixed
-            CR[l, mine, 0:64] = compress(nn3f(zk, expand(mixed)))
-            CR[l, mine, 64:65] = tops + jnp.log(total)
+            CR[l, mine] = pack(compress(nn3f(zk, expand(mixed))), [top + jnp.log(total)])
             from_owner(CR.at[l], csem_s.at[l], csem_r.at[l], True)
 
         edges(VX.at[l], vsem_s.at[l], vsem_r.at[l], "wait")
@@ -1075,148 +1108,150 @@
             DQ[b * L : (b + 1) * L, j * 128 : (j + 1) * 128] = conv(TT.at[l], VX.at[l], u)
         for u in range(U):
             b, j = unit(u)
-            to_owner_sent(u, 72, xsem_s.at[l], xsem_r.at[l])
+            to_owner_sent(u, 80, xsem_s.at[l], xsem_r.at[l])
             owner_came(CR.at[l], u, csem_s.at[l], csem_r.at[l])
             at = (slice(b * L, (b + 1) * L), slice(j * 128, (j + 1) * 128))
-            context = nn3f(RW[l, u], expand(CR[l, u, 0:64])) + DQ[at]
+            context = nn(RW[l, u].astype(BF16), expand_low(CR[l, u, 0:64])) + DQ[at]
             CTX[(l,) + at] = context.astype(BF16)
+        start_all(right_copies(l, 1, CTX.at[l], out_ranges))
 
         @pl.when(is_owner)
         def _():
             from_owner(CR.at[l], csem_s.at[l], csem_r.at[l], False)
 
         copies[1].wait()
-        HS[e % 2] = nn(CTX[l], WO[l]).astype(BF16)
+        wait_all(left_copies(l, 0, LSH, LTH.at[l]))
+        HS[e % 2] = nn(CTX[l, 0:R], WO[l]).astype(BF16)
         c = swap(e)
         c.start()
         c.wait()
-        total1 = HID[...] + both(e) + vec[l, 2:3, 0:D]
+        total1 = HID[...] + both(e) + obias[l].astype(F32)[0:1]
         T1[l] = total1
-        normed = moments(total1)[0] * vec[l, 4:5, 0:D] + vec[l, 6:7, 0:D]
+        normed = moments(total1)[0] * ngain[l].astype(F32)[0:1] + nshift[l].astype(F32)[0:1]
         HID[...] = normed
-        NL[l] = normed.astype(BF16)
+        LOW[...] = normed.astype(BF16)
+        left_put(LOW[...], LSN, LTN.at[l])
+        start_all(left_copies(l, 2, LSN, LTN.at[l]))
         copies[2].wait()
 
         def grow(i, _):
             o = pl.ds(pl.multiple_of(i * 256, 256), 256)
-            pre = nn(NL[l], WI[l, :, o]) + vec[l, 1:2, o]
+            pre = nn(LOW[...], WI[l, :, o]) + ibias[l : l + 1, o].astype(F32)
             below = 0.5 * (1.0 + lax.erf(pre * (0.5**0.5)))
-            ACT[l, :, o] = (pre * below).astype(BF16)
+            ACT[l, 0:R, o] = (pre * below).astype(BF16)
             GP[l, :, o] = (below + pre * jnp.exp(-0.5 * pre * pre) * 0.3989422804014327).astype(BF16)
             return 0
 
         lax.fori_loop(0, F // 256, grow, 0)
+        start_all(right_copies(l, 3, ACT.at[l], ffn_ranges))
         copies[3].wait()
 
         def shrink(i, _):
             o = pl.ds(pl.multiple_of(i * 256, 256), 256)
-            HS[(e + 1) % 2, :, o] = nn(ACT[l], WF[l, :, o]).astype(BF16)
+            HS[(e + 1) % 2, :, o] = nn(ACT[l, 0:R], WF[l, :, o]).astype(BF16)
             return 0
 
         lax.fori_loop(0, D // 256, shrink, 0)
         c = swap(e + 1)
         c.start()
         c.wait()
-        total2 = HID[...] + both(e + 1) + vec[l, 3:4, 0:D]
+        total2 = HID[...] + both(e + 1) + obias[l].astype(F32)[1:2]
         T2[l] = total2
-        HID[...] = moments(total2)[0] * vec[l, 5:6, 0:D] + vec[l, 7:8, 0:D]
+        wait_all(right_copies(l, 1, CTX.at[l], out_ranges))
+        wait_all(left_copies(l, 2, LSN, LTN.at[l]))
+        wait_all(right_copies(l, 3, ACT.at[l], ffn_ranges))
+        HID[...] = moments(total2)[0] * ngain[l].astype(F32)[1:2] + nshift[l].astype(F32)[1:2]
 
     def backward(l, left):
         e = 2 * z.layers + 2 * (z.layers - 1 - l)
+        k = z.layers + l
         base = 60 * l
-        total2, sums = norm_back(T2[l], UP[...], vec[l, 5:6, 0:D])
+        total2, sums = norm_back(T2[l], UP[...], ngain[l].astype(F32)[1:2])
         put_small(base + 6, sums[0])
         put_small(base + 18, sums[1])
         put_small(base + 30, sums[2])
         DT[...] = total2
         FL[...] = total2.astype(BF16)
+        left_put(FL[...], LSF, LTF)
+        feed_copies = left_copies(l, 4, LSF, LTF)
+        start_all(feed_copies)
 
         def widen(i, _):
             o = pl.ds(pl.multiple_of(i * 256, 256), 256)
             grad = nt(FL[...], WF[l, o, :]).astype(BF16).astype(F32)
             pre = (GP[l, :, o].astype(F32) * grad).astype(BF16)
-            DPRE[:, o] = pre
+            DPRE[0:R, o] = pre
             s = jnp.sum(pre.astype(F32), axis=0, keepdims=True)
             SM[pl.ds(base + 36 + 2 * i, 1), :] = s[:, 0:128]
             SM[pl.ds(base + 37 + 2 * i, 1), :] = s[:, 128:256]
             return 0
 
         lax.fori_loop(0, F // 256, widen, 0)
+        pre_copies = right_copies(l, 5, DPRE, ffn_ranges)
+        start_all(pre_copies)
 
         def narrow(i, _):
             o = pl.ds(pl.multiple_of(i * 256, 256), 256)
-            HS[e % 2, :, o] = nt(DPRE[...], WI[l, o, :]).astype(BF16)
+            HS[e % 2, :, o] = nt(DPRE[0:R], WI[l, o, :]).astype(BF16)
             return 0
 
         lax.fori_loop(0, D // 256, narrow, 0)
         c = swap(e)
         c.start()
-        for done in left[:1]:
-            done()
-        feed_t = FL[...].T
-        norm_t = NL[l].T
-        for h in range(2):
-            name = f"outer{h}"
-            weight_grad(feed_t, lambda o: ACT[l, :, pl.ds(h * FH + o, 256)], items[name][0], FH, 256)
-            rs_start(l, name, 0)
-        for h in range(2):
-            name = f"inner{h}"
-            weight_grad(norm_t, lambda o: DPRE[:, pl.ds(h * FH + o, 256)], items[name][0], FH, 256)
-            rs_start(l, name, 0)
         c.wait()
         grad_normed = DT[...] + both(e)
-        total1, sums = norm_back(T1[l], grad_normed, vec[l, 4:5, 0:D])
+        total1, sums = norm_back(T1[l], grad_normed, ngain[l].astype(F32)[0:1])
         put_small(base + 0, sums[0])
         put_small(base + 12, sums[1])
         put_small(base + 24, sums[2])
         DT[...] = total1
-        attend = total1.astype(BF16)
-        FL[...] = attend
-        grads = nt(attend, WO[l]).astype(BF16)
+        FL[...] = total1.astype(BF16)
+        grads = nt(FL[...], WO[l]).astype(BF16)
         for b in range(B):
             GX[b, margin : margin + L, :] = grads[b * L : (b + 1) * L]
         edge_zeros(GX)
-        edges(GX, vsem_s.at[z.layers + l], vsem_r.at[z.layers + l], "start")
+        edges(GX, vsem_s.at[k], vsem_r.at[k], "start")
 
         def g_tile(u):
             b, j = unit(u)
             return GX[b, margin : margin + L, j * 128 : (j + 1) * 128]
 
         for u in range(U):
-            g = g_tile(u)
-            x = tn(jnp.concatenate(halves(RW[l, u]), axis=0), jnp.concatenate([g, g], axis=0))
-            XM[u, 0:64] = compress(x)
-            to_owner(u, 64, xsem_s.at[z.layers + l], xsem_r.at[z.layers + l])
+            XM[u, 0:64] = compress(tn(RW[l, u].astype(BF16), g_tile(u))).astype(BF16)
+            to_owner(u, 64, xsem_s.at[k], xsem_r.at[k])
             DQM[u] = jnp.zeros((64, 128), F32)
+        left_put(FL[...], LSA, LTA)
+        attend_copies = left_copies(l, 6, LSA, LTA)
+        start_all(attend_copies)
+        for done in left[:1]:
+            done()
+        wait_all(feed_copies)
+        for g in range(2):
+            weight_grad(g, LTF, lambda o: ACT[l, :, pl.ds(g * FH + o, 256)], items["outer"][0], FH, 256)
+        rs_start(l, "outer", 0)
+
+        @pl.when(is_owner)
+        def _():
+            owner_gets(64, xsem_s.at[k], xsem_r.at[k])
+            d_core = OB[0, 0:64].astype(F32)
+            for i in range(1, n):
+                d_core = d_core + OB[i, 0:64].astype(F32)
+            PC[...] = d_core
+            d_mixed = tn3f(PZ[l], expand(d_core))
+            off = jnp.sum(d_mixed * expand(MX[l]), axis=1, keepdims=True)
+            DR[mine] = pack(compress(d_mixed), [to_row(off)])
+            from_owner(DR, csem_s.at[k], csem_r.at[k], True)
+
         for u in range(U):
             b, j = unit(u)
             at = (slice(b * L, (b + 1) * L), slice(j * 128, (j + 1) * 128))
-            g = g_tile(u)
-            core_pair = halves(expand(CR[l, u, 0:64]))
-            d_row = nt(jnp.concatenate([g, g], axis=1), jnp.concatenate(core_pair, axis=1))
+            d_row = nt(g_tile(u), expand_low(CR[l, u, 0:64]))
             rw = RW[l, u]
-            d_rs = halves(rw * (d_row - half_sums(rw * d_row)))
-            DQ[at] = nn3(d_rs, halves(expand(KM[l, u])))
-            DKM[u] = compress(tn3(d_rs, pair_tile(QS, l, u)))
-
-        for done in left[1:2]:
-            done()
-        advance(l, ("outer0", "outer1"), 0)
-
-        @pl.when(is_owner)
-        def _():
-            owner_gets(64, xsem_s.at[z.layers + l], xsem_r.at[z.layers + l])
-            d_core = OB[0, 0:64]
-            for i in range(1, n):
-                d_core = d_core + OB[i, 0:64]
-            PC[...] = d_core
-            d_mixed = tn3f(PZ[l], expand(d_core))
-            DR[mine, 0:64] = compress(d_mixed)
-            DR[mine, 64:65] = to_row(jnp.sum(d_mixed * expand(MX[l]), axis=1, keepdims=True))
-            from_owner(DR, csem_s.at[z.layers + l], csem_r.at[z.layers + l], True)
-
+            d_rs = (rw * (d_row - half_sums(rw * d_row))).astype(BF16)
+            DQ[at] = nn(d_rs, expand(KM[l, u]).astype(BF16))
+            DKM[u] = compress(tn(d_rs, pair_tile(QS, l, u)[0]))
         for u in range(U):
-            to_owner_sent(u, 64, xsem_s.at[z.layers + l], xsem_r.at[z.layers + l])
+            to_owner_sent(u, 64, xsem_s.at[k], xsem_r.at[k])
 
         @pl.when(is_owner)
         def _():
@@ -1259,9 +1294,13 @@
             DQM[mine] = compress(nn3(d_ms, halves(expand(KM[l, mine]))))
             DKM[mine] = DKM[mine] + compress(tn3(d_ms, halves(expand(QM[l, mine]))))
 
-        advance(l, ("inner0", "inner1"), 0)
-        advance(l, ("outer0", "outer1"), 1)
-        edges(GX, vsem_s.at[z.layers + l], vsem_r.at[z.layers + l], "wait")
+        for done in left[1:2]:
+            done()
+        wait_all(pre_copies)
+        for g in range(2):
+            weight_grad(g, LTN.at[l], lambda o: DPRE[:, pl.ds(g * FH + o, 256)], items["inner"][0], FH, 256)
+        rs_start(l, "inner", 0)
+        edges(GX, vsem_s.at[k], vsem_r.at[k], "wait")
         for u in range(U):
             b, j = unit(u)
             at = (slice(b * L, (b + 1) * L), slice(j * 128, (j + 1) * 128))
@@ -1276,43 +1315,51 @@
                 found = pltpu.roll(found, 129, 1, stride=1, stride_axis=0)
                 row = base + 54 + 2 * j + h
                 SM[row : row + 1, :] = jnp.sum(found[:, 0:128], axis=0, keepdims=True)
+        advance(l, "outer", 0)
         for u in range(U):
             b, j = unit(u)
             at = (slice(b * L, (b + 1) * L), slice(j * 128, (j + 1) * 128))
-            owner_came(DR, u, csem_s.at[z.layers + l], csem_r.at[z.layers + l])
-            qbh = halves(expand(QM[l, u]))
-            dmh = halves(expand(DR[u, 0:64]))
-            off = to_col(DR[u, 64:65])
-            kw = jnp.exp(KSC[l, u] - to_col(CR[l, u, 64:65]))
+            owner_came(DR, u, csem_s.at[k], csem_r.at[k])
+            dm = expand_low(DR[u, 0:64])
+            off = to_col(packed_row(DR.at[u], 0))
+            kw = jnp.exp(KSC[l, u] - to_col(packed_row(CR.at[l, u], 0)))
             v = VX[l, b, margin : margin + L, j * 128 : (j + 1) * 128]
-            DV[at] = DV[at] + tn3(halves(kw), dmh)
-            d_kw = nt(jnp.concatenate(dmh, axis=1), jnp.concatenate([v, v], axis=1))
-            d_ks = halves(kw * (d_kw - off))
-            DK[at] = tn3(d_ks, qbh)
-            DQM[u] = DQM[u] + compress(nn3(d_ks, pair_tile(KS, l, u)))
+            DV[at] = DV[at] + tn(kw.astype(BF16), dm)
+            d_ks = (kw * (nt(dm, v) - off)).astype(BF16)
+            DK[at] = tn(d_ks, expand(QM[l, u]).astype(BF16))
+            DQM[u] = DQM[u] + compress(nn(d_ks, pair_tile(KS, l, u)[0]))
 
         @pl.when(is_owner)
         def _():
-            from_owner(DR, csem_s.at[z.layers + l], csem_r.at[z.layers + l], False)
-
-        advance(l, ("inner0", "inner1"), 1)
-        for done in left[2:3]:
-            done()
+            from_owner(DR, csem_s.at[k], csem_r.at[k], False)
+
         for u in range(U):
             b, j = unit(u)
             lanes = slice(j * 128, (j + 1) * 128)
+            dq, dk = DQM[u].astype(BF16), DKM[u].astype(BF16)
             for i in range(n):
-                SB[i, b * S : (b + 1) * S, lanes] = DQM[u, i * S : (i + 1) * S]
-                SB[i, 8 + b * S : 8 + (b + 1) * S, lanes] = DKM[u, i * S : (i + 1) * S]
+                SB[i, b * S : (b + 1) * S, lanes] = dq[i * S : (i + 1) * S]
+                SB[i, 8 + b * S : 8 + (b + 1) * S, lanes] = dk[i * S : (i + 1) * S]
+        for done in left[2:]:
+            done()
+        DP[0:R, 2 * C : 3 * C] = DV[...].astype(BF16)
+        value_copies = right_copies(l, 7, DP, val_ranges)
+        wait_all(attend_copies)
+        out0 = items["outval"][0]
+        weight_grad(0, LTA, lambda o: CTX[l, :, pl.ds(o, 128)], out0, 128, 128)
+        weight_grad(1, LTA, lambda o: CTX[l, :, pl.ds(128 + o, 256)], out0, C - 128, 256)
         spread(lambda t: SB.at[t], SR, qsem_s.at[l], qsem_r.at[l], True)
         SR[me] = SB[me]
-        advance(l, ("outer0", "outer1"), 2)
-        for done in left[3:]:
-            done()
+        start_all(value_copies)
+        advance(l, "inner", 0)
+        wait_all(value_copies)
+        weight_grad(0, LTH.at[l], lambda o: DP[:, pl.ds(2 * C + o, 256)], out0 + 128, C - 128, 256)
+        weight_grad(1, LTH.at[l], lambda o: DP[:, pl.ds(3 * C - 128 + o, 128)], out0 + C - 128, 128, 128)
+        rs_start(l, "outval", 0)
         spread(lambda t: SB.at[t], SR, qsem_s.at[l], qsem_r.at[l], False)
-        marks = SR[0]
+        marks = SR[0].astype(F32)
         for i in range(1, n):
-            marks = marks + SR[i]
+            marks = marks + SR[i].astype(F32)
         marks = marks * (1.0 / z.segment)
         for b in range(B):
             for r in range(S):
@@ -1320,154 +1367,167 @@
                 i = b * S + r
                 DP[at, 0:C] = ((DQ[at] + marks[i : i + 1]) * scale).astype(BF16)
                 DP[at, C : 2 * C] = ((DK[at] + marks[8 + i : 9 + i]) * scale).astype(BF16)
-        DP[:, 2 * C : 3 * C] = DV[...].astype(BF16)
+        key_copies = right_copies(l, 8, DP, key_ranges)
+        start_all(key_copies)
 
         def onto(i, _):
             o = pl.ds(pl.multiple_of(i * 256, 256), 256)
-            x = nt(DP[:, 0:C], WP[l, 0, o, :]) + nt(DP[:, C : 2 * C], WP[l, 1, o, :])
-            HS[(e + 1) % 2, :, o] = (x + nt(DP[:, 2 * C : 3 * C], WP[l, 2, o, :])).astype(BF16)
+            x = nt(DP[0:R, 0:C], WP[l, 0, o, :]) + nt(DP[0:R, C : 2 * C], WP[l, 1, o, :])
+            HS[(e + 1) % 2, :, o] = (x + nt(DP[0:R, 2 * C : 3 * C], WP[l, 2, o, :])).astype(BF16)
             return 0
 
         lax.fori_loop(0, D // 256, onto, 0)
         c = swap(e + 1)
         c.start()
-        bias = jnp.sum(DP[...].astype(F32), axis=0, keepdims=True)
+        bias = jnp.sum(DP[0:R].astype(F32), axis=0, keepdims=True)
         put_small(base + 48, bias[:, 0:C])
         put_small(base + 51, bias[:, 2 * C : 3 * C])
-        attend_t = FL[...].T
-        hidden_t = HL[l].T
-        t0, t1 = items["tail0"][0], items["tail1"][0]
-        weight_grad(attend_t, lambda o: CTX[l, :, pl.ds(o, 128)], t0, 128, 128)
-        weight_grad(hidden_t, lambda o: DP[:, pl.ds(o, 128)], t0 + 128, C, 128)
-        weight_grad(hidden_t, lambda o: DP[:, pl.ds(2 * C + o, 256)], t0 + 128 + C, 256, 256)
-        rs_start(l, "tail0", 0)
-        weight_grad(attend_t, lambda o: CTX[l, :, pl.ds(128 + o, 256)], t1, C - 128, 256)
-        weight_grad(hidden_t, lambda o: DP[:, pl.ds(C + o, 128)], t1 + C - 128, C, 128)
-        weight_grad(hidden_t, lambda o: DP[:, pl.ds(2 * C + 256 + o, 128)], t1 + 2 * C - 128, C - 256, 128)
-        rs_start(l, "tail1", 0)
+        advance(l, "outer", 1)
+        wait_all(key_copies)
+        for g in range(2):
+            weight_grad(g, LTH.at[l], lambda o: DP[:, pl.ds(g * C + o, 128)], items["keyed"][0], C, 128)
+        rs_start(l, "keyed", 0)
         c.wait()
         UP[...] = DT[...] + both(e + 1)
-        advance(l, ("inner0", "inner1"), 2)
-        advance(l, ("outer0", "outer1"), 3)
-
-    def advance(l, names, stage):
-        for name in names:
-            rs_add(l, name, stage)
-            if stage + 1 < NB:
-                rs_start(l, name, stage + 1)
 
     for l in range(z.layers):
         forward(l)
-    result[...] = HID[...]
-    pltpu.make_async_copy(ups, UP, wsem.at[0, 4]).wait()
+    for b in range(B):
+        result[b] = HID[b * L : (b + 1) * L, :]
+        shown = to_col(mask[b : b + 1, :].astype(F32))
+        UP[b * L : (b + 1) * L, :] = cot[b].astype(F32) * shown
     left = []
     for l in range(z.layers - 1, -1, -1):
         backward(l, left)
-        left = [
-            partial(advance, l, ("inner0", "inner1"), 3),
-        ] + [partial(advance, l, ("tail0", "tail1"), s) for s in range(NB)]
-    gtok[...] = UP[...]
+
+        def rest(l=l):
+            advance(l, "inner", 1)
+            advance(l, "outval", 0)
+            advance(l, "outer", 2)
+
+        def more(l=l):
+            advance(l, "inner", 2)
+            advance(l, "keyed", 0)
+            advance(l, "outval", 1)
+
+        def last(l=l):
+            advance(l, "keyed", 1)
+            advance(l, "outval", 2)
+            advance(l, "keyed", 2)
+
+        left = [rest, more, last]
+    for b in range(B):
+        gtok[b] = UP[b * L : (b + 1) * L, :]
     spread(lambda t: SM.at[pl.ds(pl.multiple_of(t * 8, 8), 8)], SMR, ssem_s, ssem_r, True)
     SMR[me] = SM[pl.ds(pl.multiple_of(me * 8, 8), 8), :]
     left[0]()
-    left[1]()
     spread(lambda t: SM.at[pl.ds(pl.multiple_of(t * 8, 8), 8)], SMR, ssem_s, ssem_r, False)
     total = SMR[0]
     for i in range(1, n):
         total = total + SMR[i]
     SMT[me] = total
     spread(lambda t: SMT.at[me], SMT, tsem_s, tsem_r, True)
-    for done in left[2:]:
-        done()
+    left[1]()
+    left[2]()
     spread(lambda t: SMT.at[me], SMT, tsem_s, tsem_r, False)
-    for i in range(n):
-        gsmall[i * 8 : (i + 1) * 8, :] = SMT[i]
+
+    def small(at):
+        return SMT[at // 8, at % 8 : at % 8 + 1, :]
+
+    for l in range(z.layers):
+        base = 60 * l
+        for i in range(D // 128):
+            lanes = slice(i * 128, (i + 1) * 128)
+            for side in range(2):
+                ggain[l, side : side + 1, lanes] = small(base + 6 * side + i)
+                gshift[l, side : side + 1, lanes] = small(base + 12 + 6 * side + i)
+                gobias[l, side : side + 1, lanes] = small(base + 24 + 6 * side + i)
+        for i in range(F // 128):
+            gibias[l : l + 1, i * 128 : (i + 1) * 128] = small(base + 36 + i)
+        for i in range(C // 128):
+            gbias[l, 0:1, i * 128 : (i + 1) * 128] = small(base + 48 + i)
+            gbias[l, 1:2, i * 128 : (i + 1) * 128] = small(base + 51 + i)
+        for h in range(z.local_heads):
+            gtaps[l, h : h + 1, :] = small(base + 54 + h)[:, 0:K]
+
+
+def hand_over(count, *refs):
+    sems = refs[-1]
+    copies = [
+        pltpu.make_async_copy(refs[i], refs[count + i], sems.at[i]) for i in range(count)
+    ]
+    for c in copies:
+        c.start()
+    for c in copies:
+        c.wait()
 
 
 def fused(z, tokens, cotangent, masked, projections, projection_bias, conv_taps, output_weight,
           output_bias, norm_gain, norm_shift, inner_weight, inner_bias, outer_weight):
     n, B, L, R, D, C, F = z.n, z.batch, z.length, z.rows, z.width, z.cols, z.hidden
     U, H, NL_, NB, CH = z.units, z.local_heads, z.layers, z.bits, z.width // z.n
-    wide = max(F, 2 * C, D)
-
-    def padded(x):
-        return jnp.pad(x.astype(F32), [(0, 0)] * (x.ndim - 1) + [(0, wide - x.shape[-1])])
-
-    vec = jnp.concatenate(
-        [
-            padded(projection_bias.reshape(NL_, 1, 2 * C)),
-            padded(inner_bias[:, None]),
-            padded(output_bias),
-            padded(norm_gain),
-            padded(norm_shift),
-        ],
-        axis=1,
-    )
-    taps = jnp.stack([conv_taps, conv_taps[:, :, ::-1]], axis=1).astype(F32)
-    taps = jnp.pad(taps, ((0, 0), (0, 0), (0, 8 - H), (0, 256 - z.kernel)))
-    ups = (cotangent.astype(F32) * masked.astype(F32)[:, :, None]).reshape(R, D)
     V = pltpu.VMEM
     DMA = pltpu.SemaphoreType.DMA
-    cols = 2 * F + 4 * C
+    cols = F + 2 * C
+    staged = lambda: V((2,) * NB + (CH, R), BF16)
+    gathered = lambda *lead: V(lead + (2,) * NB + (CH, 2 * R), BF16)
     scratch = dict(
         WP=V((NL_, 3, D, C), BF16), WO=V((NL_, C, D), BF16), WI=V((NL_, D, F), BF16), WF=V((NL_, F, D), BF16),
-        HL=V((NL_, R, D), BF16), QS=V((NL_, 2, R, C), BF16), KS=V((NL_, 2, R, C), BF16),
+        QS=V((NL_, 2, R, C), BF16), KS=V((NL_, 2, R, C), BF16),
         VX=V((NL_, B, 256, C), BF16), RW=V((NL_, U, 128, 128), F32), KSC=V((NL_, U, 128, 128), F32),
-        CTX=V((NL_, R, C), BF16), T1=V((NL_, R, D), F32), T2=V((NL_, R, D), F32), NL=V((NL_, R, D), BF16),
-        GP=V((NL_, R, F), BF16), ACT=V((NL_, R, F), BF16),
-        QM=V((NL_, U, 64, 128), F32), KM=V((NL_, U, 64, 128), F32), CR=V((NL_, U, 72, 128), F32),
+        CTX=V((NL_, 2 * R, C), BF16), T1=V((NL_, R, D), F32), T2=V((NL_, R, D), F32),
+        GP=V((NL_, R, F), BF16), ACT=V((NL_, 2 * R, F), BF16),
+        QM=V((NL_, U, 64, 128), F32), KM=V((NL_, U, 64, 128), F32), CR=V((NL_, U, 80, 128), BF16),
         MX=V((NL_, 64, 128), F32), PA=V((NL_, 128, 128), F32), PV=V((NL_, PINV_ITERS, 4, 128, 128), F32),
-        PZ=V((NL_, 128, 128), F32), PC=V((64, 128), F32),
-        HID=V((R, D), F32), UP=V((R, D), F32), DT=V((R, D), F32), FL=V((R, D), BF16), DPRE=V((R, F), BF16),
-        GX=V((B, 256, C), BF16), DQ=V((R, C), F32), DK=V((R, C), F32), DV=V((R, C), F32), DP=V((R, 3 * C), BF16),
-        DQM=V((U, 64, 128), F32), DKM=V((U, 64, 128), F32), DR=V((U, 72, 128), F32), SM=V((n * 8, 128), F32),
-        TT=V((NL_, H, 128, 256), BF16), TR=V((NL_, H, 128, 256), BF16),
-        MS=V((16, C), F32), MB=V((n, 16, C), F32), XM=V((U, 72, 128), F32), OB=V((n, 72, 128), F32),
-        SB=V((n, 16, C), F32), SR=V((n, 16, C), F32), HS=V((2, R, D), BF16), HR=V((2, R, D), BF16),
+        PZ=V((NL_, 128, 128), F32), PC=V((64, 128), F32), LTH=gathered(NL_), LTN=gathered(NL_),
+        HID=V((R, D), F32), UP=V((R, D), F32), LOW=V((R, D), BF16),
+        DPRE=V((2 * R, F), BF16), GX=V((B, 256, C), BF16), DQ=V((R, C), F32), DK=V((R, C), F32), DV=V((R, C), F32),
+        DP=V((2 * R, 3 * C), BF16), DQM=V((U, 64, 128), F32), DKM=V((U, 64, 128), F32), DR=V((U, 80, 128), BF16),
+        SM=V((n * 8, 128), F32), TB=V((2, 8, 256), F32),
+        TT=V((NL_, H, 128, 256), BF16), TR=V((NL_, H, 128, 256), BF16), LTF=gathered(), LTA=gathered(),
+        LSH=staged(), LSN=staged(),
+        MS=V((16, C), F32), MB=V((n, 16, C), F32), XM=V((U, 80, 128), BF16), OB=V((n, 80, 128), BF16),
+        SB=V((n, 16, C), BF16), SR=V((n, 16, C), BF16), HS=V((2, R, D), BF16), HR=V((2, R, D), BF16),
         SMR=V((n, 8, 128), F32), SMT=V((n, 8, 128), F32),
         G=V((2,) * NB + (CH, cols), BF16),
-        RV=[V((1 if s < 2 else NL_,) + (2,) * (NB - 1 - s) + (CH, cols), BF16) for s in range(NB)],
-        wsem=DMA((NL_, 5)),
+        RV=[V((NL_, 2) + (2,) * (NB - 2 - s) + (CH, cols), BF16) for s in range(NB - 1)],
+        wsem=DMA((NL_, 4)),
         hsem_s=DMA((4 * NL_,)), hsem_r=DMA((4 * NL_,)),
         msem_s=DMA((NL_, n)), msem_r=DMA((NL_, n)), xsem_s=DMA((2 * NL_, U)), xsem_r=DMA((2 * NL_, n)),
         csem_s=DMA((2 * NL_, n)), csem_r=DMA((2 * NL_, U)), vsem_s=DMA((2 * NL_, 2)), vsem_r=DMA((2 * NL_, 2)),
-        gsem_s=DMA((NL_, 6, NB)), gsem_r=DMA((NL_, 6, NB)), qsem_s=DMA((NL_, n)), qsem_r=DMA((NL_, n)),
+        asem_s=DMA((NL_, 9, 2)), asem_r=DMA((NL_, 9, 2)),
+        gsem_s=DMA((NL_, 4, 2, NB - 1)), gsem_r=DMA((NL_, 4, 2, NB - 1)), qsem_s=DMA((NL_, n)), qsem_r=DMA((NL_, n)),
         ssem_s=DMA((n,)), ssem_r=DMA((n,)), tsem_s=DMA((n,)), tsem_r=DMA((n,)),
     )
     in_vmem = pl.BlockSpec(memory_space=pltpu.VMEM)
     in_hbm = pl.BlockSpec(memory_space=pl.ANY)
     out = lambda *s: jax.ShapeDtypeStruct(s, F32)
+    shapes = (
+        out(B, L, D), out(B, L, D), out(NL_, 3, CH, C), out(NL_, 2, C), out(NL_, H, z.kernel), out(NL_, CH, C),
+        out(NL_, 2, D), out(NL_, 2, D), out(NL_, 2, D), out(NL_, CH, F), out(NL_, F), out(NL_, CH, F),
+    )
     outs = pl.pallas_call(
         partial(fused_kernel, z),
-        out_shape=(
-            out(R, D), out(R, D), out(NL_, 3, CH, C), out(NL_, CH, C), out(NL_, CH, F), out(NL_, CH, F),
-            out(n * 8, 128),
-        ),
-        in_specs=[in_vmem, in_hbm, in_vmem, in_vmem] + [in_hbm] * 4,
-        out_specs=(in_vmem,) * 7,
+        out_shape=shapes,
+        in_specs=[in_vmem] * 9 + [in_hbm] * 4,
+        out_specs=(in_vmem,) * len(shapes),
         scratch_shapes=scratch,
         compiler_params=pltpu.CompilerParams(
             collective_id=1, has_side_effects=True, vmem_limit_bytes=VMEM_LIMIT
         ),
-    )(tokens.reshape(R, D), ups, vec, taps, projections, output_weight, inner_weight, outer_weight)
-    result, gtok, gproj, gout, ginner, gouter, small = outs
-    small = small[: 60 * NL_].reshape(NL_, 60, 128)
-
-    def pair(at):
-        return small[:, at : at + 2 * (D // 128)].reshape(NL_, 2, D)
-
-    k = D // 128
-    gain, shift, bias = pair(0), pair(2 * k), pair(4 * k)
-    at = 6 * k
-    grad_inner_bias = small[:, at : at + F // 128].reshape(NL_, F)
-    at += F // 128
-    grad_bias = small[:, at : at + 2 * C // 128].reshape(NL_, 2, C)
-    at += 2 * C // 128
-    grad_taps = small[:, at : at + H, : z.kernel]
-    return (
-        result.reshape(B, L, D), gtok.reshape(B, L, D), gproj, grad_bias, grad_taps,
-        jnp.swapaxes(gout, 1, 2), bias, gain, shift, ginner, grad_inner_bias, jnp.swapaxes(gouter, 1, 2),
-    )
+    )(tokens, cotangent, masked, projection_bias, conv_taps, output_bias, norm_gain, norm_shift, inner_bias,
+      projections, output_weight, inner_weight, outer_weight)
+    outs = list(
+        pl.pallas_call(
+            partial(hand_over, len(shapes)),
+            out_shape=shapes,
+            in_specs=[in_vmem] * len(shapes),
+            out_specs=(in_hbm,) * len(shapes),
+            scratch_shapes=[DMA((len(shapes),))],
+        )(*outs)
+    )
+    outs[5], outs[11] = jnp.swapaxes(outs[5], 1, 2), jnp.swapaxes(outs[11], 1, 2)
+    return tuple(outs)
 
 
 def solution(mesh):

time: 317 us -> 238 us (0.75)
  Pallas kernels: 295 us -> 235 us
  local copies, waits for them, and re-layouts: 17.2 us -> 2.57 us
  other arithmetic: 3.97 us -> 0 us
    pallas_call x1 -> x2, Pallas kernels: 295 us -> 235 us  [the longest x1 231 us: fused(): pl.pallas_call(partial(fused_kernel, z), out_shape=shapes, in_specs=[in_v...]
    unnamed x16 -> x2, local copies, waits for them, and re-layouts: 10.1 us -> 2.57 us
where the time goes in v2:
time: 238 us
  Pallas kernels  235 us (99%)
  local copies, waits for them, and re-layouts  2.57 us (1%)
    pallas_call x1, Pallas kernels, fused(): pl.pallas_call(partial(fused_kernel, z), out_shape=shapes, in_specs=[in_v...  231 us

profile of v2, /device:TPU:0, one launch (start us, length us, event | category | flops | bytes accessed | tf_op | source)
XLA Modules:
  0.0 238.0 jit_solution(3572711675550683483)
XLA Ops:
  0.6 1.3 copy.25.taps
  1.9 231.0 %shard_map.220 = (f32[2,128,768]{2,1,0:T(8,128)}, f32[2,128,768]{2,1,0:T(8,128)}, f32[2,3,48,384]{3,2,1,0:T(8,128)}, f32[2,2,384]{2,1,0:T(2,128)}, f32[2,6,65]{2...) custom-call(bf16[2,128,768]{2,1,0:T(8,128)(2,1)} %tok.1, ...), custom_call_target="tpu_custom_call" | custom-call | tf_op jit(solution)/shard_map/pallas_call | solution.py:1509
  232.9 3.8 %shard_map.221 = (f32[2,128,768]{2,1,0:T(8,128)}, f32[2,128,768]{2,1,0:T(8,128)}, f32[2,3,48,384]{3,2,1,0:T(8,128)}, f32[2,2,384]{2,1,0:T(2,128)}, f32[2,6,65]{2...) custom-call(f32[2,128,768]{2,1,0:T(8,128)} %get-tuple-element.36.ref, ...), custom_call_target="tpu_custom_call" | custom-call | tf_op jit(solution)/shard_map/pallas_call | solution.py:1521
  236.8 1.3 copy.26

commit v3 on v2

--- a/solution.py
+++ b/solution.py
@@ -608,13 +608,13 @@
     result, gtok, gproj, gbias, gtaps, gout, gobias, ggain, gshift, ginner, gibias, gouter,
     *,
     WP, WO, WI, WF,
-    QS, KS, VX, RW, KSC, CTX, T1, T2, GP, ACT, QM, KM, CR, MX, PA, PV, PZ, PC, LTH, LTN,
-    HID, UP, LOW, DPRE, GX, DQ, DK, DV, DP, DQM, DKM, DR, SM, TB, TT, TR, LTF, LTA,
-    LSH, LSN,
-    MS, MB, XM, OB, SB, SR, HS, HR, SMR, SMT,
+    QS, KS, VX, RW, CTX, T1, T2, GP, ACT, QM, KM, CR, MX, PA, PV, PZ, PC, LTH, LTN,
+    HID, UP, LOW, PN, PF, DPRE, GX, DQ, DK, DV, DP, DQM, DKM, DR, SM, TB, TT, TR, LTF, LTA,
+    LSH, OP, OO, OI, OU, OS, OT,
+    MS, MB, MD, MO, XM, OB, SB, SR, HS, HR, SMR, SMT,
     G, RV,
-    wsem, hsem_s, hsem_r, msem_s, msem_r, xsem_s, xsem_r, csem_s, csem_r, vsem_s, vsem_r,
-    asem_s, asem_r, gsem_s, gsem_r, qsem_s, qsem_r, ssem_s, ssem_r, tsem_s, tsem_r,
+    wsem, hsem_s, hsem_r, msem_s, msem_r, dsem_s, dsem_r, xsem_s, xsem_r, csem_s, csem_r, vsem_s, vsem_r,
+    osem, asem_s, asem_r, bsem_s, bsem_r, gsem_s, gsem_r, qsem_s, qsem_r, ssem_s, ssem_r, tsem_s, tsem_r,
 ):
     n, B, L, R, D, C, F = z.n, z.batch, z.length, z.rows, z.width, z.cols, z.hidden
     U, NP, S, K = z.units, z.local_heads // 2, z.spans, z.kernel
@@ -637,9 +637,7 @@
             pltpu.make_async_copy(wf_hbm.at[l], WF.at[l], wsem.at[l, 3]),
         ]
 
-    for l in range(z.layers):
-        for c in weight_copies(l):
-            c.start()
+    weight_copies(0)[0].start()
 
     barrier = pltpu.get_barrier_semaphore()
 
@@ -651,7 +649,6 @@
 
     lax.fori_loop(1, n, greet, 0)
     pl.semaphore_signal(barrier, inc=1, device_id={"head": 1 - core}, device_id_type=MESH)
-    pl.semaphore_wait(barrier, n)
 
     row_id = lax.broadcasted_iota(jnp.int32, (128, 128), 0)
     lane_id = lax.broadcasted_iota(jnp.int32, (128, 128), 1)
@@ -710,12 +707,6 @@
     def tile(ref, l, u):
         b, j = unit(u)
         return ref[l, b * L : (b + 1) * L, j * 128 : (j + 1) * 128]
-
-    def pair_tile(ref, l, u):
-        b, j = unit(u)
-        return tuple(
-            ref[l, p, b * L : (b + 1) * L, j * 128 : (j + 1) * 128] for p in range(2)
-        )
 
     def moments(x):
         centre = jnp.mean(x, -1, keepdims=True)
@@ -770,34 +761,30 @@
 
         lax.fori_loop(1, n, step if start else finish, 0)
 
-    def to_owner(u, rows, ss, rs):
-        c = pltpu.make_async_remote_copy(
-            XM.at[u, pl.ds(0, rows)], OB.at[me, pl.ds(0, rows)], ss.at[u], rs.at[me],
-            device_id={"seq": first_owner + u}, device_id_type=MESH,
+    def to_owner_copy(u, src, dst, ss, rs):
+        return pltpu.make_async_remote_copy(
+            src, dst.at[me], ss.at[u], rs.at[me], device_id={"seq": first_owner + u}, device_id_type=MESH
         )
 
+    def to_owner(u, src, dst, ss, rs):
         @pl.when(me != first_owner + u)
         def _():
-            c.start()
+            to_owner_copy(u, src, dst, ss, rs).start()
 
         @pl.when(me == first_owner + u)
         def _():
-            OB[me, 0:rows] = XM[u, 0:rows]
-
-    def to_owner_sent(u, rows, ss, rs):
+            dst[me] = src[...]
+
+    def to_owner_sent(u, src, dst, ss, rs):
         @pl.when(me != first_owner + u)
         def _():
-            pltpu.make_async_remote_copy(
-                XM.at[u, pl.ds(0, rows)], OB.at[me, pl.ds(0, rows)], ss.at[u], rs.at[me],
-                device_id={"seq": first_owner + u}, device_id_type=MESH,
-            ).wait_send()
-
-    def owner_gets(rows, ss, rs):
+            to_owner_copy(u, src, dst, ss, rs).wait_send()
+
+    def owner_gets(src, dst, ss, rs):
         def step(d, _):
             t = lax.rem(me + d, n)
             pltpu.make_async_remote_copy(
-                XM.at[0, pl.ds(0, rows)], OB.at[t, pl.ds(0, rows)], ss.at[0], rs.at[t],
-                device_id={"seq": t}, device_id_type=MESH,
+                src, dst.at[t], ss.at[0], rs.at[t], device_id={"seq": t}, device_id_type=MESH
             ).wait_recv()
             return 0
 
@@ -871,7 +858,7 @@
         x = buf[b, :, j * 128 : (j + 1) * 128]
         return jnp.where(low_lane, nn(bands[2 * j], x), nn(bands[2 * j + 1], x))
 
-    DT, FL, LSF, LSA = HID, LOW, LSH, LSN
+    DT, FL = HID, LOW
     own_bits = [lax.rem(me // (1 << k), 2) for k in range(NB)]
     dims = [[k for k in reversed(range(NB)) if k != g] for g in range(2)]
     FH = F // 2
@@ -898,21 +885,56 @@
     def left_copies(l, i, stage, gathered):
         got = []
         for g in range(2):
-            at = [everything] * NB
+            at = [core] + [everything] * (NB - 1)
             at[NB - 1 - g] = 1 - own_bits[g]
             src = stage.at[tuple(at) + (pl.ds(0, CH), pl.ds(0, R))]
-            dst = gathered.at[(g,) + (everything,) * (NB - 1) + (pl.ds(0, CH), pl.ds(R, R))]
+            dst = gathered.at[(g, core) + (everything,) * (NB - 2) + (pl.ds(0, CH), pl.ds(R, R))]
             got.append(pair_copy(l, i, g, src, dst))
         return got
+
+    def core_copy(l, i, g, ref):
+        return pltpu.make_async_remote_copy(
+            ref, ref, bsem_s.at[l, i, g], bsem_r.at[l, i, g],
+            device_id={"head": 1 - core}, device_id_type=MESH,
+        )
+
+    def left_hand_on(l, i, gathered):
+        return [
+            core_copy(l, i, g, gathered.at[(g, core) + (everything,) * (NB - 2) + (pl.ds(0, CH), pl.ds(R, R))])
+            for g in range(2)
+        ]
+
+    def row_copies(l, i, src, dst):
+        at = pl.ds(pl.multiple_of(core * L, L), L)
+        return [pair_copy(l, i, g, src.at[at], dst.at[g, at]) for g in range(2)]
+
+    def row_hand_on(l, i, dst):
+        at = pl.ds(pl.multiple_of(core * L, L), L)
+        return [core_copy(l, i, g, dst.at[g, at]) for g in range(2)]
+
+    def each_half(g, act):
+        for code in range(n // 2):
+            spot = tuple((code >> (NB - 2 - i)) & 1 for i in range(NB - 1))
+            at = list(spot)
+            at.insert(NB - 1 - g, own_bits[g])
+            act((g,) + spot, tuple(at))
 
     def left_put(x, stage, gathered):
         stage[...] = x.T.reshape(stage.shape)
         for g in range(2):
-            for code in range(n // 2):
-                spot = tuple((code >> (NB - 2 - i)) & 1 for i in range(NB - 1))
-                at = list(spot)
-                at.insert(NB - 1 - g, own_bits[g])
-                gathered[(g,) + spot + (slice(None), slice(0, R))] = stage[tuple(at)]
+            def put(to, at):
+                gathered[to + (slice(None), slice(0, R))] = stage[at]
+
+            each_half(g, put)
+
+    def left_put_theirs(rows, stage, gathered):
+        for g in range(2):
+            stage[...] = rows[g].T.reshape(stage.shape)
+
+            def put(to, at):
+                gathered[to + (slice(None), slice(R, 2 * R))] = stage[at]
+
+            each_half(g, put)
 
     def start_all(copies):
         for c in copies:
@@ -970,17 +992,20 @@
 
     def write_out(l, name, g, x):
         if name == "outer":
-            gouter[l, :, g * FH : (g + 1) * FH] = x
+            OU[l, :, g * FH : (g + 1) * FH] = x
         elif name == "inner":
-            ginner[l, :, g * FH : (g + 1) * FH] = x
+            OI[l, :, g * FH : (g + 1) * FH] = x
         elif name == "keyed":
-            gproj[l, g] = x
+            OP[l, g] = x
         elif g == 0:
-            gout[l, :, 0:128] = x[:, 0:128]
-            gproj[l, 2, :, 0 : C - 128] = x[:, 128:C]
+            OO[l, :, 0:128] = x[:, 0:128]
+            OP[l, 2, :, 0 : C - 128] = x[:, 128:C]
         else:
-            gout[l, :, 128:C] = x[:, 0 : C - 128]
-            gproj[l, 2, :, C - 128 : C] = x[:, C - 128 : C]
+            OO[l, :, 128:C] = x[:, 0 : C - 128]
+            OP[l, 2, :, C - 128 : C] = x[:, C - 128 : C]
+
+    def out_copy(i, src, dst):
+        return pltpu.make_async_copy(src, dst, osem.at[i])
 
     def advance(l, name, stage):
         rs_add(l, name, stage)
@@ -995,69 +1020,119 @@
     for b in range(B):
         HID[b * L : (b + 1) * L, :] = tok[b].astype(F32)
     TB[...] = jnp.zeros_like(TB)
-    backwards = jnp.where(row_id + lane_id == K - 1, 1.0, 0.0).astype(BF16)
-    for l in range(z.layers):
+
+    def make_bands(l):
+        backwards = jnp.where(row_id + lane_id == K - 1, 1.0, 0.0).astype(BF16)
         TB[0, 0 : z.local_heads, 0:K] = taps[l].astype(F32)
         TB[1, :, 0:128] = nn(TB[0, :, 0:128].astype(BF16), backwards)
-        for h in range(z.local_heads):
-            for which, store in ((0, TT), (1, TR)):
+        for which, store in ((0, TT), (1, TR)):
+            for h in range(z.local_heads):
                 base = jnp.broadcast_to(TB[which, h : h + 1, :], (128, 256))
                 store[l, h] = pltpu.roll(base, 0, 1, stride=1, stride_axis=0).astype(BF16)
+
+    def regrow(l):
+        wait_all(row_hand_on(l, 2, PN))
+        left_put_theirs(PN, LSH, LTN.at[l])
+        for g in range(2):
+            def step(i, _):
+                o = pl.ds(pl.multiple_of(g * FH + i * 256, 256), 256)
+                act, slope = unit_rows(PN[g], l, o)
+                ACT[l, R : 2 * R, o] = act
+                GP[l, R : 2 * R, o] = slope
+                return 0
+
+            lax.fori_loop(0, FH // 256, step, 0)
+
+    def unit_rows(rows, l, o):
+        pre = nn(rows, WI[l, :, o]) + ibias[l : l + 1, o].astype(F32)
+        below = 0.5 * (1.0 + lax.erf(pre * (0.5**0.5)))
+        slope = below + pre * jnp.exp(-0.5 * pre * pre) * 0.3989422804014327
+        return (pre * below).astype(BF16), slope.astype(BF16)
 
     def forward(l):
         copies = weight_copies(l)
         e = 2 * l
-        hl = HID[...].astype(BF16)
-        LOW[...] = hl
+        LOW[...] = HID[...].astype(BF16)
         copies[0].wait()
+        if l == 0:
+            for c in [weight_copies(0)[i] for i in (1, 2, 3)] + weight_copies(1):
+                c.start()
         both_bias = pbias[l].astype(F32)
         bias_q, bias_v = both_bias[0:1], both_bias[1:2]
-        q = (nn(hl, WP[l, 0]) + bias_q) * scale
-        k = nn(hl, WP[l, 1]) * scale
-        QS[l, 0], QS[l, 1] = halves(q)
-        KS[l, 0], KS[l, 1] = halves(k)
-        for b in range(B):
-            for r in range(S):
-                at = b * L + r * z.segment
-                i = b * S + r
-                MS[i : i + 1, :] = jnp.sum(q[at : at + z.segment], axis=0, keepdims=True) * (1.0 / z.segment)
-                MS[8 + i : 9 + i, :] = jnp.sum(k[at : at + z.segment], axis=0, keepdims=True) * (1.0 / z.segment)
+        q = (nn(LOW[...], WP[l, 0]) + bias_q) * scale
+        k = nn(LOW[...], WP[l, 1]) * scale
+        QS[l] = q.astype(BF16)
+        KS[l] = k.astype(BF16)
+        sums = []
+        for x in (q, k):
+            for b in range(B):
+                for r in range(S):
+                    at = b * L + r * z.segment
+                    sums.append(jnp.sum(x[at : at + z.segment], axis=0, keepdims=True))
+        marks = jnp.concatenate(sums, axis=0) * (1.0 / z.segment)
+        MS[...] = marks.astype(BF16)
+        rest = marks - MS[...].astype(F32)
+        middle = rest.astype(BF16).astype(F32)
+        rest = rest - middle
+        for u in range(U):
+            b, j = unit(u)
+            parts = [
+                x[first + b * S : first + (b + 1) * S, j * 128 : (j + 1) * 128]
+                for x in (middle, rest)
+                for first in (0, 8)
+            ]
+            MD[u] = jnp.concatenate(parts, axis=0).astype(BF16)
+        if l == 0:
+            pl.semaphore_wait(barrier, n)
         spread(lambda t: MS, MB, msem_s.at[l], msem_r.at[l], True)
+        for u in range(U):
+            to_owner(u, MD.at[u], MO, dsem_s.at[l], dsem_r.at[l])
         MB[me] = MS[...]
-        vl = (nn(hl, WP[l, 2]) + bias_v).astype(BF16)
+        vl = (nn(LOW[...], WP[l, 2]) + bias_v).astype(BF16)
         for b in range(B):
             VX[l, b, margin : margin + L, :] = vl[b * L : (b + 1) * L]
         edge_zeros(VX.at[l])
         edges(VX.at[l], vsem_s.at[l], vsem_r.at[l], "start")
+        if l:
+            regrow(l - 1)
         left_put(LOW[...], LSH, LTH.at[l])
-        spread(lambda t: MS, MB, msem_s.at[l], msem_r.at[l], False)
+        make_bands(l)
+        edges(VX.at[l], vsem_s.at[l], vsem_r.at[l], "wait")
         for u in range(U):
             b, j = unit(u)
-            for i in range(n):
-                at = slice(i * S, (i + 1) * S)
-                QM[l, u, at, :] = MB[i, b * S : (b + 1) * S, j * 128 : (j + 1) * 128]
-                KM[l, u, at, :] = MB[i, 8 + b * S : 8 + (b + 1) * S, j * 128 : (j + 1) * 128]
+            DQ[b * L : (b + 1) * L, j * 128 : (j + 1) * 128] = conv(TT.at[l], VX.at[l], u)
+        spread(lambda t: MS, MB, msem_s.at[l], msem_r.at[l], False)
+        hidden_copies = left_copies(l, 0, LSH, LTH.at[l])
+        start_all(hidden_copies)
         for u in range(U):
             b, j = unit(u)
-            qb = expand(QM[l, u])
-            ksc = nt3(halves(qb), pair_tile(KS, l, u))
-            KSC[l, u] = ksc
+            lanes = slice(j * 128, (j + 1) * 128)
+            for first, store in ((0, QM), (8, KM)):
+                rows = [MB[i, :, lanes].astype(F32)[first + b * S : first + (b + 1) * S] for i in range(n)]
+                store[l, u] = jnp.concatenate(rows, axis=0)
+        for u in range(U):
+            b, j = unit(u)
+            ksc = nt(expand(QM[l, u]).astype(BF16), tile(KS, l, u))
             top = jnp.max(ksc, axis=1, keepdims=True)
             p = jnp.exp(ksc - top)
             total = jnp.sum(p, axis=1, keepdims=True)
             v = VX[l, b, margin : margin + L, j * 128 : (j + 1) * 128]
             XM[u] = pack(compress(nn(p.astype(BF16), v)), [to_row(top), to_row(total)])
-            to_owner(u, 80, xsem_s.at[l], xsem_r.at[l])
-        start_all(left_copies(l, 0, LSH, LTH.at[l]))
+            to_owner(u, XM.at[u], OB, xsem_s.at[l], xsem_r.at[l])
         for u in range(U):
-            kb = expand(KM[l, u])
-            s = nt3(pair_tile(QS, l, u), halves(kb))
+            s = nt(tile(QS, l, u), expand(KM[l, u]).astype(BF16))
             p = jnp.exp(s - half_tops(s))
             RW[l, u] = p / half_sums(p)
 
         @pl.when(is_owner)
         def _():
-            qb, kb = expand(QM[l, mine]), expand(KM[l, mine])
+            owner_gets(MD.at[0], MO, dsem_s.at[l], dsem_r.at[l])
+            extra = []
+            for i in range(n):
+                x = MO[i].astype(F32)
+                extra.append(x[0:8] + x[8:16])
+            qb = expand(QM[l, mine] + jnp.concatenate([x[0:S] for x in extra], axis=0))
+            kb = expand(KM[l, mine] + jnp.concatenate([x[S : 2 * S] for x in extra], axis=0))
             s = jnp.where(same_head, nt3f(qb, kb), -jnp.inf)
             p = jnp.exp(s - jnp.max(s, axis=1, keepdims=True))
             a = p / jnp.sum(p, axis=1, keepdims=True)
@@ -1085,7 +1160,7 @@
 
             zk = lax.fori_loop(0, PINV_ITERS, iterate, a.T / tops)
             PZ[l] = zk
-            owner_gets(80, xsem_s.at[l], xsem_r.at[l])
+            owner_gets(XM.at[0], OB, xsem_s.at[l], xsem_r.at[l])
             tops = [packed_row(OB.at[i], 0) for i in range(n)]
             top = tops[0]
             for i in range(1, n):
@@ -1102,13 +1177,12 @@
             CR[l, mine] = pack(compress(nn3f(zk, expand(mixed))), [top + jnp.log(total)])
             from_owner(CR.at[l], csem_s.at[l], csem_r.at[l], True)
 
-        edges(VX.at[l], vsem_s.at[l], vsem_r.at[l], "wait")
+        wait_all(hidden_copies)
+        start_all(left_hand_on(l, 0, LTH.at[l]))
         for u in range(U):
             b, j = unit(u)
-            DQ[b * L : (b + 1) * L, j * 128 : (j + 1) * 128] = conv(TT.at[l], VX.at[l], u)
-        for u in range(U):
-            b, j = unit(u)
-            to_owner_sent(u, 80, xsem_s.at[l], xsem_r.at[l])
+            to_owner_sent(u, XM.at[u], OB, xsem_s.at[l], xsem_r.at[l])
+            to_owner_sent(u, MD.at[u], MO, dsem_s.at[l], dsem_r.at[l])
             owner_came(CR.at[l], u, csem_s.at[l], csem_r.at[l])
             at = (slice(b * L, (b + 1) * L), slice(j * 128, (j + 1) * 128))
             context = nn(RW[l, u].astype(BF16), expand_low(CR[l, u, 0:64])) + DQ[at]
@@ -1120,7 +1194,6 @@
             from_owner(CR.at[l], csem_s.at[l], csem_r.at[l], False)
 
         copies[1].wait()
-        wait_all(left_copies(l, 0, LSH, LTH.at[l]))
         HS[e % 2] = nn(CTX[l, 0:R], WO[l]).astype(BF16)
         c = swap(e)
         c.start()
@@ -1130,20 +1203,18 @@
         normed = moments(total1)[0] * ngain[l].astype(F32)[0:1] + nshift[l].astype(F32)[0:1]
         HID[...] = normed
         LOW[...] = normed.astype(BF16)
-        left_put(LOW[...], LSN, LTN.at[l])
-        start_all(left_copies(l, 2, LSN, LTN.at[l]))
+        norm_copies = row_copies(l, 2, LOW, PN)
+        start_all(norm_copies)
         copies[2].wait()
 
         def grow(i, _):
             o = pl.ds(pl.multiple_of(i * 256, 256), 256)
-            pre = nn(LOW[...], WI[l, :, o]) + ibias[l : l + 1, o].astype(F32)
-            below = 0.5 * (1.0 + lax.erf(pre * (0.5**0.5)))
-            ACT[l, 0:R, o] = (pre * below).astype(BF16)
-            GP[l, :, o] = (below + pre * jnp.exp(-0.5 * pre * pre) * 0.3989422804014327).astype(BF16)
+            act, slope = unit_rows(LOW[...], l, o)
+            ACT[l, 0:R, o] = act
+            GP[l, 0:R, o] = slope
             return 0
 
         lax.fori_loop(0, F // 256, grow, 0)
-        start_all(right_copies(l, 3, ACT.at[l], ffn_ranges))
         copies[3].wait()
 
         def shrink(i, _):
@@ -1154,13 +1225,13 @@
         lax.fori_loop(0, D // 256, shrink, 0)
         c = swap(e + 1)
         c.start()
+        left_put(LOW[...], LSH, LTN.at[l])
         c.wait()
         total2 = HID[...] + both(e + 1) + obias[l].astype(F32)[1:2]
         T2[l] = total2
-        wait_all(right_copies(l, 1, CTX.at[l], out_ranges))
-        wait_all(left_copies(l, 2, LSN, LTN.at[l]))
-        wait_all(right_copies(l, 3, ACT.at[l], ffn_ranges))
         HID[...] = moments(total2)[0] * ngain[l].astype(F32)[1:2] + nshift[l].astype(F32)[1:2]
+        wait_all(norm_copies)
+        start_all(row_hand_on(l, 2, PN))
 
     def backward(l, left):
         e = 2 * z.layers + 2 * (z.layers - 1 - l)
@@ -1172,14 +1243,13 @@
         put_small(base + 30, sums[2])
         DT[...] = total2
         FL[...] = total2.astype(BF16)
-        left_put(FL[...], LSF, LTF)
-        feed_copies = left_copies(l, 4, LSF, LTF)
+        feed_copies = row_copies(l, 4, FL, PF)
         start_all(feed_copies)
 
         def widen(i, _):
             o = pl.ds(pl.multiple_of(i * 256, 256), 256)
             grad = nt(FL[...], WF[l, o, :]).astype(BF16).astype(F32)
-            pre = (GP[l, :, o].astype(F32) * grad).astype(BF16)
+            pre = (GP[l, 0:R, o].astype(F32) * grad).astype(BF16)
             DPRE[0:R, o] = pre
             s = jnp.sum(pre.astype(F32), axis=0, keepdims=True)
             SM[pl.ds(base + 36 + 2 * i, 1), :] = s[:, 0:128]
@@ -1187,9 +1257,6 @@
             return 0
 
         lax.fori_loop(0, F // 256, widen, 0)
-        pre_copies = right_copies(l, 5, DPRE, ffn_ranges)
-        start_all(pre_copies)
-
         def narrow(i, _):
             o = pl.ds(pl.multiple_of(i * 256, 256), 256)
             HS[e % 2, :, o] = nt(DPRE[0:R], WI[l, o, :]).astype(BF16)
@@ -1198,6 +1265,11 @@
         lax.fori_loop(0, D // 256, narrow, 0)
         c = swap(e)
         c.start()
+        left_put(FL[...], LSH, LTF)
+        if l == z.layers - 1:
+            regrow(l)
+        wait_all(feed_copies)
+        start_all(row_hand_on(l, 4, PF))
         c.wait()
         grad_normed = DT[...] + both(e)
         total1, sums = norm_back(T1[l], grad_normed, ngain[l].astype(F32)[0:1])
@@ -1218,21 +1290,30 @@
 
         for u in range(U):
             XM[u, 0:64] = compress(tn(RW[l, u].astype(BF16), g_tile(u))).astype(BF16)
-            to_owner(u, 64, xsem_s.at[k], xsem_r.at[k])
+            to_owner(u, XM.at[u, pl.ds(0, 64)], OB.at[:, pl.ds(0, 64)], xsem_s.at[k], xsem_r.at[k])
             DQM[u] = jnp.zeros((64, 128), F32)
-        left_put(FL[...], LSA, LTA)
-        attend_copies = left_copies(l, 6, LSA, LTA)
+        wait_all(row_hand_on(l, 4, PF))
+        left_put_theirs(PF, LSH, LTF)
+        for g in range(2):
+            def step(i, _):
+                o = pl.ds(pl.multiple_of(g * FH + i * 256, 256), 256)
+                grad = nt(PF[g], WF[l, o, :]).astype(BF16).astype(F32)
+                DPRE[R : 2 * R, o] = (GP[l, R : 2 * R, o].astype(F32) * grad).astype(BF16)
+                return 0
+
+            lax.fori_loop(0, FH // 256, step, 0)
+        left_put(FL[...], LSH, LTA)
+        attend_copies = left_copies(l, 6, LSH, LTA)
         start_all(attend_copies)
         for done in left[:1]:
             done()
-        wait_all(feed_copies)
         for g in range(2):
             weight_grad(g, LTF, lambda o: ACT[l, :, pl.ds(g * FH + o, 256)], items["outer"][0], FH, 256)
         rs_start(l, "outer", 0)
 
         @pl.when(is_owner)
         def _():
-            owner_gets(64, xsem_s.at[k], xsem_r.at[k])
+            owner_gets(XM.at[0, pl.ds(0, 64)], OB.at[:, pl.ds(0, 64)], xsem_s.at[k], xsem_r.at[k])
             d_core = OB[0, 0:64].astype(F32)
             for i in range(1, n):
                 d_core = d_core + OB[i, 0:64].astype(F32)
@@ -1249,9 +1330,9 @@
             rw = RW[l, u]
             d_rs = (rw * (d_row - half_sums(rw * d_row))).astype(BF16)
             DQ[at] = nn(d_rs, expand(KM[l, u]).astype(BF16))
-            DKM[u] = compress(tn(d_rs, pair_tile(QS, l, u)[0]))
+            DKM[u] = compress(tn(d_rs, tile(QS, l, u)))
         for u in range(U):
-            to_owner_sent(u, 64, xsem_s.at[k], xsem_r.at[k])
+            to_owner_sent(u, XM.at[u, pl.ds(0, 64)], OB.at[:, pl.ds(0, 64)], xsem_s.at[k], xsem_r.at[k])
 
         @pl.when(is_owner)
         def _():
@@ -1296,7 +1377,8 @@
 
         for done in left[1:2]:
             done()
-        wait_all(pre_copies)
+        wait_all(attend_copies)
+        start_all(left_hand_on(l, 6, LTA))
         for g in range(2):
             weight_grad(g, LTN.at[l], lambda o: DPRE[:, pl.ds(g * FH + o, 256)], items["inner"][0], FH, 256)
         rs_start(l, "inner", 0)
@@ -1322,12 +1404,13 @@
             owner_came(DR, u, csem_s.at[k], csem_r.at[k])
             dm = expand_low(DR[u, 0:64])
             off = to_col(packed_row(DR.at[u], 0))
-            kw = jnp.exp(KSC[l, u] - to_col(packed_row(CR.at[l, u], 0)))
+            qb = expand(QM[l, u]).astype(BF16)
+            kw = jnp.exp(nt(qb, tile(KS, l, u)) - to_col(packed_row(CR.at[l, u], 0)))
             v = VX[l, b, margin : margin + L, j * 128 : (j + 1) * 128]
             DV[at] = DV[at] + tn(kw.astype(BF16), dm)
             d_ks = (kw * (nt(dm, v) - off)).astype(BF16)
-            DK[at] = tn(d_ks, expand(QM[l, u]).astype(BF16))
-            DQM[u] = DQM[u] + compress(nn(d_ks, pair_tile(KS, l, u)[0]))
+            DK[at] = tn(d_ks, qb)
+            DQM[u] = DQM[u] + compress(nn(d_ks, tile(KS, l, u)))
 
         @pl.when(is_owner)
         def _():
@@ -1344,7 +1427,8 @@
             done()
         DP[0:R, 2 * C : 3 * C] = DV[...].astype(BF16)
         value_copies = right_copies(l, 7, DP, val_ranges)
-        wait_all(attend_copies)
+        wait_all(left_hand_on(l, 6, LTA))
+        wait_all(right_copies(l, 1, CTX.at[l], out_ranges))
         out0 = items["outval"][0]
         weight_grad(0, LTA, lambda o: CTX[l, :, pl.ds(o, 128)], out0, 128, 128)
         weight_grad(1, LTA, lambda o: CTX[l, :, pl.ds(128 + o, 256)], out0, C - 128, 256)
@@ -1353,6 +1437,7 @@
         start_all(value_copies)
         advance(l, "inner", 0)
         wait_all(value_copies)
+        wait_all(left_hand_on(l, 0, LTH.at[l]))
         weight_grad(0, LTH.at[l], lambda o: DP[:, pl.ds(2 * C + o, 256)], out0 + 128, C - 128, 256)
         weight_grad(1, LTH.at[l], lambda o: DP[:, pl.ds(3 * C - 128 + o, 128)], out0 + C - 128, 128, 128)
         rs_start(l, "outval", 0)
@@ -1392,10 +1477,12 @@
 
     for l in range(z.layers):
         forward(l)
+    results = [out_copy(b, HID.at[pl.ds(b * L, L)], result.at[b]) for b in range(B)]
+    start_all(results)
     for b in range(B):
-        result[b] = HID[b * L : (b + 1) * L, :]
         shown = to_col(mask[b : b + 1, :].astype(F32))
         UP[b * L : (b + 1) * L, :] = cot[b].astype(F32) * shown
+    wait_all(results)
     left = []
     for l in range(z.layers - 1, -1, -1):
         backward(l, left)
@@ -1416,8 +1503,8 @@
             advance(l, "keyed", 2)
 
         left = [rest, more, last]
-    for b in range(B):
-        gtok[b] = UP[b * L : (b + 1) * L, :]
+    tokens_out = [out_copy(B + b, UP.at[pl.ds(b * L, L)], gtok.at[b]) for b in range(B)]
+    start_all(tokens_out)
     spread(lambda t: SM.at[pl.ds(pl.multiple_of(t * 8, 8), 8)], SMR, ssem_s, ssem_r, True)
     SMR[me] = SM[pl.ds(pl.multiple_of(me * 8, 8), 8), :]
     left[0]()
@@ -1428,10 +1515,11 @@
     SMT[me] = total
     spread(lambda t: SMT.at[me], SMT, tsem_s, tsem_r, True)
     left[1]()
-    left[2]()
+    ffn_out = [out_copy(2 * B, OU, gouter), out_copy(2 * B + 1, OI, ginner)]
+    start_all(ffn_out)
     spread(lambda t: SMT.at[me], SMT, tsem_s, tsem_r, False)
 
-    def small(at):
+    def little(at):
         return SMT[at // 8, at % 8 : at % 8 + 1, :]
 
     for l in range(z.layers):
@@ -1439,16 +1527,26 @@
         for i in range(D // 128):
             lanes = slice(i * 128, (i + 1) * 128)
             for side in range(2):
-                ggain[l, side : side + 1, lanes] = small(base + 6 * side + i)
-                gshift[l, side : side + 1, lanes] = small(base + 12 + 6 * side + i)
-                gobias[l, side : side + 1, lanes] = small(base + 24 + 6 * side + i)
+                for what in range(3):
+                    OS[what, l, side : side + 1, lanes] = little(base + 12 * what + 6 * side + i)
         for i in range(F // 128):
-            gibias[l : l + 1, i * 128 : (i + 1) * 128] = small(base + 36 + i)
+            OT[l : l + 1, i * 128 : (i + 1) * 128] = little(base + 36 + i)
         for i in range(C // 128):
-            gbias[l, 0:1, i * 128 : (i + 1) * 128] = small(base + 48 + i)
-            gbias[l, 1:2, i * 128 : (i + 1) * 128] = small(base + 51 + i)
+            gbias[l, 0:1, i * 128 : (i + 1) * 128] = little(base + 48 + i)
+            gbias[l, 1:2, i * 128 : (i + 1) * 128] = little(base + 51 + i)
         for h in range(z.local_heads):
-            gtaps[l, h : h + 1, :] = small(base + 54 + h)[:, 0:K]
+            gtaps[l, h : h + 1, :] = little(base + 54 + h)[:, 0:K]
+    small_out = [
+        out_copy(2 * B + 2 + i, src, dst)
+        for i, (src, dst) in enumerate(
+            [(OS.at[0], ggain), (OS.at[1], gshift), (OS.at[2], gobias), (OT, gibias)]
+        )
+    ]
+    start_all(small_out)
+    left[2]()
+    rest_out = [out_copy(2 * B + 6, OP, gproj), out_copy(2 * B + 7, OO, gout)]
+    start_all(rest_out)
+    wait_all(tokens_out + ffn_out + small_out + rest_out)
 
 
 def hand_over(count, *refs):
@@ -1473,29 +1571,31 @@
     gathered = lambda *lead: V(lead + (2,) * NB + (CH, 2 * R), BF16)
     scratch = dict(
         WP=V((NL_, 3, D, C), BF16), WO=V((NL_, C, D), BF16), WI=V((NL_, D, F), BF16), WF=V((NL_, F, D), BF16),
-        QS=V((NL_, 2, R, C), BF16), KS=V((NL_, 2, R, C), BF16),
-        VX=V((NL_, B, 256, C), BF16), RW=V((NL_, U, 128, 128), F32), KSC=V((NL_, U, 128, 128), F32),
+        QS=V((NL_, R, C), BF16), KS=V((NL_, R, C), BF16),
+        VX=V((NL_, B, 256, C), BF16), RW=V((NL_, U, 128, 128), F32),
         CTX=V((NL_, 2 * R, C), BF16), T1=V((NL_, R, D), F32), T2=V((NL_, R, D), F32),
-        GP=V((NL_, R, F), BF16), ACT=V((NL_, 2 * R, F), BF16),
+        GP=V((NL_, 2 * R, F), BF16), ACT=V((NL_, 2 * R, F), BF16),
         QM=V((NL_, U, 64, 128), F32), KM=V((NL_, U, 64, 128), F32), CR=V((NL_, U, 80, 128), BF16),
         MX=V((NL_, 64, 128), F32), PA=V((NL_, 128, 128), F32), PV=V((NL_, PINV_ITERS, 4, 128, 128), F32),
         PZ=V((NL_, 128, 128), F32), PC=V((64, 128), F32), LTH=gathered(NL_), LTN=gathered(NL_),
-        HID=V((R, D), F32), UP=V((R, D), F32), LOW=V((R, D), BF16),
+        HID=V((R, D), F32), UP=V((R, D), F32), LOW=V((R, D), BF16), PN=V((2, R, D), BF16), PF=V((2, R, D), BF16),
         DPRE=V((2 * R, F), BF16), GX=V((B, 256, C), BF16), DQ=V((R, C), F32), DK=V((R, C), F32), DV=V((R, C), F32),
         DP=V((2 * R, 3 * C), BF16), DQM=V((U, 64, 128), F32), DKM=V((U, 64, 128), F32), DR=V((U, 80, 128), BF16),
         SM=V((n * 8, 128), F32), TB=V((2, 8, 256), F32),
         TT=V((NL_, H, 128, 256), BF16), TR=V((NL_, H, 128, 256), BF16), LTF=gathered(), LTA=gathered(),
-        LSH=staged(), LSN=staged(),
-        MS=V((16, C), F32), MB=V((n, 16, C), F32), XM=V((U, 80, 128), BF16), OB=V((n, 80, 128), BF16),
+        LSH=staged(), OP=V((NL_, 3, CH, C), F32), OO=V((NL_, CH, C), F32), OI=V((NL_, CH, F), F32),
+        OU=V((NL_, CH, F), F32), OS=V((3, NL_, 2, D), F32), OT=V((NL_, F), F32),
+        MS=V((16, C), BF16), MB=V((n, 16, C), BF16), MD=V((U, 16, 128), BF16), MO=V((n, 16, 128), BF16), XM=V((U, 80, 128), BF16), OB=V((n, 80, 128), BF16),
         SB=V((n, 16, C), BF16), SR=V((n, 16, C), BF16), HS=V((2, R, D), BF16), HR=V((2, R, D), BF16),
         SMR=V((n, 8, 128), F32), SMT=V((n, 8, 128), F32),
         G=V((2,) * NB + (CH, cols), BF16),
         RV=[V((NL_, 2) + (2,) * (NB - 2 - s) + (CH, cols), BF16) for s in range(NB - 1)],
         wsem=DMA((NL_, 4)),
         hsem_s=DMA((4 * NL_,)), hsem_r=DMA((4 * NL_,)),
-        msem_s=DMA((NL_, n)), msem_r=DMA((NL_, n)), xsem_s=DMA((2 * NL_, U)), xsem_r=DMA((2 * NL_, n)),
+        msem_s=DMA((NL_, n)), msem_r=DMA((NL_, n)), dsem_s=DMA((NL_, U)), dsem_r=DMA((NL_, n)), xsem_s=DMA((2 * NL_, U)), xsem_r=DMA((2 * NL_, n)),
         csem_s=DMA((2 * NL_, n)), csem_r=DMA((2 * NL_, U)), vsem_s=DMA((2 * NL_, 2)), vsem_r=DMA((2 * NL_, 2)),
-        asem_s=DMA((NL_, 9, 2)), asem_r=DMA((NL_, 9, 2)),
+        osem=DMA((2 * B + 8,)),
+        asem_s=DMA((NL_, 9, 2)), asem_r=DMA((NL_, 9, 2)), bsem_s=DMA((NL_, 9, 2)), bsem_r=DMA((NL_, 9, 2)),
         gsem_s=DMA((NL_, 4, 2, NB - 1)), gsem_r=DMA((NL_, 4, 2, NB - 1)), qsem_s=DMA((NL_, n)), qsem_r=DMA((NL_, n)),
         ssem_s=DMA((n,)), ssem_r=DMA((n,)), tsem_s=DMA((n,)), tsem_r=DMA((n,)),
     )
@@ -1510,7 +1610,7 @@
         partial(fused_kernel, z),
         out_shape=shapes,
         in_specs=[in_vmem] * 9 + [in_hbm] * 4,
-        out_specs=(in_vmem,) * len(shapes),
+        out_specs=tuple(in_vmem if i in (3, 4) else in_hbm for i in range(len(shapes))),
         scratch_shapes=scratch,
         compiler_params=pltpu.CompilerParams(
             collective_id=1, has_side_effects=True, vmem_limit_bytes=VMEM_LIMIT
@@ -1526,7 +1626,8 @@
             scratch_shapes=[DMA((len(shapes),))],
         )(*outs)
     )
-    outs[5], outs[11] = jnp.swapaxes(outs[5], 1, 2), jnp.swapaxes(outs[11], 1, 2)
+    for i in (5, 11):
+        outs[i] = jnp.swapaxes(outs[i], 1, 2)
     return tuple(outs)
 
 

time: 238 us -> 202 us (0.85)
  Pallas kernels: 235 us -> 199 us
    pallas_call x1, Pallas kernels: 231 us -> 195 us  [fused(): pl.pallas_call(partial(fused_kernel, z), out_shape=shapes, in_specs=[in_v...]
where the time goes in v3:
time: 202 us
  Pallas kernels  199 us (99%)
  local copies, waits for them, and re-layouts  2.57 us (1%)
    pallas_call x1, Pallas kernels, fused(): pl.pallas_call(partial(fused_kernel, z), out_shape=shapes, in_specs=[in_v...  195 us

profile of v3, /device:TPU:0, one launch (start us, length us, event | category | flops | bytes accessed | tf_op | source)
XLA Modules:
  0.0 202.1 jit_solution(4673430618018111919)
XLA Ops:
  0.6 1.3 copy.25.taps
  1.9 195.1 %shard_map.220 = (f32[2,128,768]{2,1,0:T(8,128)}, f32[2,128,768]{2,1,0:T(8,128)}, f32[2,3,48,384]{3,2,1,0:T(8,128)}, f32[2,2,384]{2,1,0:T(2,128)}, f32[2,6,65]{2...) custom-call(bf16[2,128,768]{2,1,0:T(8,128)(2,1)} %tok.1, ...), custom_call_target="tpu_custom_call" | custom-call | tf_op jit(solution)/shard_map/pallas_call | solution.py:1609
  197.0 3.8 %shard_map.221 = (f32[2,128,768]{2,1,0:T(8,128)}, f32[2,128,768]{2,1,0:T(8,128)}, f32[2,3,48,384]{3,2,1,0:T(8,128)}, f32[2,2,384]{2,1,0:T(2,128)}, f32[2,6,65]{2...) custom-call(f32[2,128,768]{2,1,0:T(8,128)} %get-tuple-element.36.ref, ...), custom_call_target="tpu_custom_call" | custom-call | tf_op jit(solution)/shard_map/pallas_call | solution.py:1621
  200.8 1.3 copy.26
